TPU v7x, 32 devices: a whole 2x2x4 slice. The times are simulated.
32 devices in a mesh: grp: 2 (over core), ctx: 8 (over z, y), wsh: 2 (over x).
Axes of the slice: x: 2, y: 2, z: 4, core: 2. Of those that a mesh axis runs over, the one named last changes fastest.
Arguments:
- stream: bfloat16 [2, 2, 3072, 512], P('grp', 'wsh', 'ctx'), may hold values from -6 to 6
- memory: bfloat16 [2, 2, 1024, 512], P('grp', 'wsh', 'ctx'), may hold values from -6 to 6
- cotangent: bfloat16 [2, 2, 3072, 512], P('grp', 'wsh', 'ctx'), may hold values from -6 to 6
- deal_order: int32 [2, 2, 24], P('grp', 'wsh'), may hold values from 0 to 23, each once within a row
- offsets: int32 [2, 2, 1], P('grp', 'wsh'), may hold values from 128 to 1024
- context_mask: int32 [2, 2, 16, 8], P('grp', 'wsh'), may hold values 0 or 1
- w_qkv: bfloat16 [512, 1536], replicated, may hold values from -0.25 to 0.25
- w_out: bfloat16 [512, 512], replicated, may hold values from -3 to 3
- w_cq: bfloat16 [512, 512], replicated, may hold values from -0.25 to 0.25
- w_ckv: bfloat16 [512, 1024], replicated, may hold values from -0.25 to 0.25
- w_cout: bfloat16 [512, 512], replicated, may hold values from -3 to 3
- w_up: bfloat16 [512, 2048], replicated, may hold values from -0.25 to 0.25
- w_down: bfloat16 [2048, 512], replicated, may hold values from -0.125 to 0.125
- b_up: float32 [2048], replicated, may hold values from -3 to 3
- gains: float32 [3, 512], replicated, may hold values from 0.5 to 1.5
- biases: float32 [10, 512], replicated, may hold values from -3 to 3
Outputs:
- output: float32 [2, 2, 3072, 512], P('grp', 'wsh', 'ctx')
- grad_stream: float32 [2, 2, 3072, 512], P('grp', 'wsh', 'ctx')
- grad_memory: float32 [2, 2, 1024, 512], P('grp', 'wsh', 'ctx')
- grad_w_qkv: float32 [512, 1536], P(('ctx', 'wsh'))
- grad_w_out: float32 [512, 512], P(('ctx', 'wsh'))
- grad_w_cq: float32 [512, 512], P(('ctx', 'wsh'))
- grad_w_ckv: float32 [512, 1024], P(('ctx', 'wsh'))
- grad_w_cout: float32 [512, 512], P(('ctx', 'wsh'))
- grad_w_up: float32 [512, 2048], P(('ctx', 'wsh'))
- grad_w_down: float32 [2048, 512], P(('ctx', 'wsh'))
- grad_b_up: float32 [2048], P(('ctx', 'wsh'))
- grad_gains: float32 [3, 512], P(None, ('ctx', 'wsh'))
- grad_biases: float32 [10, 512], P(None, ('ctx', 'wsh'))
Inputs may be any that keep to these rules, and one draw needn't show every extreme that they name: `deal_order`: each family's row is a permutation of the block numbers 0 to 23.
All inputs are finite; a program needn't handle non-finite values. No bound on the sum of `context_mask` on one device may be relied on, other than what follows from the above.
Results may differ from a plain program's by a relative error of at most 0.025.
Values may be sent and summed in bfloat16 or wider, within the bound.
A program may use at most 320 MiB of HBM per device.

v0:
```python
import jax
import jax.numpy as jnp
from jax import lax
from jax.sharding import PartitionSpec as P

HEADS = 8
BLK = 128
CBLK = 16


NEG_FILL = -1000000000.0
EPS_NORM = 1e-05


def gelu_exact(values):
    return jax.nn.gelu(values, approximate=False)


def norm_rows(values, gain_vec, shift_vec):
    center = values - jnp.mean(values, axis=-1, keepdims=True)
    spread = jnp.mean(center * center, axis=-1, keepdims=True)
    return center * lax.rsqrt(spread + EPS_NORM) * gain_vec + shift_vec


def norm_back(values, gain_vec, shift_vec, upstream):
    _, pullback = jax.vjp(norm_rows, values, gain_vec, shift_vec)
    return pullback(upstream)


def seq_index(positions, prompt_len, cont_len):
    later = jnp.int32(1) + (positions - jnp.int32(prompt_len)) // jnp.int32(cont_len)
    return jnp.where(positions < prompt_len, jnp.zeros_like(later), later)


def visible(query_pos, key_ids, offsets, context_mask, block_len, prompt_blocks, cont_blocks):
    prompt_len = prompt_blocks * block_len
    cont_len = cont_blocks * block_len
    cont_count = offsets.shape[0]
    key_pos = (
        key_ids[:, None] * jnp.int32(block_len) + jnp.arange(block_len, dtype=jnp.int32)[None, :]
    ).reshape(-1)
    query_seq = seq_index(query_pos, prompt_len, cont_len)
    key_seq = seq_index(key_pos, prompt_len, cont_len)
    inside = (query_seq[:, None] == key_seq[None, :]) & (key_pos[None, :] <= query_pos[:, None])
    cont_pick = jnp.clip(query_seq - 1, 0, cont_count - 1)
    prompt_limit = jnp.take(offsets, cont_pick)
    query_block = jnp.clip(
        (query_pos - jnp.int32(prompt_len)) // jnp.int32(block_len), 0, cont_count * cont_blocks - 1
    )
    mask_rows = jnp.take(context_mask, query_block, axis=0)
    key_block = jnp.clip(key_ids, 0, prompt_blocks - 1)
    block_open = jnp.take(mask_rows, key_block, axis=1) > 0
    block_open = jnp.repeat(block_open, block_len, axis=1) | (key_pos[None, :] < block_len)
    from_prompt = (
        (query_seq[:, None] > 0)
        & (key_seq[None, :] == 0)
        & (key_pos[None, :] < prompt_limit[:, None])
        & block_open
    )
    return inside | from_prompt


def dot_first(left, right):
    return lax.dot_general(
        left, right, (((0,), (0,)), ((), ())), preferred_element_type=jnp.float32
    )


def dot_last(left, right):
    return lax.dot_general(
        left, right, (((1,), (1,)), ((), ())), preferred_element_type=jnp.float32
    )


def to_heads(matrix, head_count):
    row_count, model_width = matrix.shape
    return matrix.reshape(row_count, head_count, model_width // head_count).transpose(1, 0, 2)


def from_heads(stacked):
    head_count, row_count, head_width = stacked.shape
    return stacked.transpose(1, 0, 2).reshape(row_count, head_count * head_width)


def pair_heads(key_rows, value_rows, head_count):
    return jnp.concatenate(
        [to_heads(key_rows, head_count), to_heads(value_rows, head_count)], axis=2
    )


def head_scores(queries, key_rows, allowed):
    score_scale = queries.shape[1] ** (-0.5)
    scores = dot_last(queries, key_rows) * score_scale
    if allowed is not None:
        scores = jnp.where(allowed, scores, NEG_FILL)
    return scores


def head_forward(queries, keyval, allowed):
    head_width = queries.shape[1]
    scores = head_scores(queries, keyval[:, :head_width], allowed)
    row_top = jnp.max(scores, axis=1, keepdims=True)
    exp_scores = jnp.exp(scores - row_top)
    row_total = jnp.sum(exp_scores, axis=1, keepdims=True)
    soft_weights = (exp_scores / row_total).astype(jnp.bfloat16)
    mixed_heads = jnp.dot(soft_weights, keyval[:, head_width:], preferred_element_type=jnp.float32)
    return (mixed_heads, row_top + jnp.log(row_total))


def head_backward(queries, keyval, upstream, log_total, allowed):
    head_width = queries.shape[1]
    score_scale = head_width ** (-0.5)
    key_rows = keyval[:, :head_width]
    scores = head_scores(queries, key_rows, allowed)
    soft_weights = jnp.exp(scores - log_total)
    grad_soft = dot_last(upstream, keyval[:, head_width:])
    row_delta = jnp.sum(soft_weights * grad_soft, axis=1, keepdims=True)
    grad_scores = (soft_weights * (grad_soft - row_delta)).astype(jnp.bfloat16)
    grad_query = jnp.dot(grad_scores, key_rows, preferred_element_type=jnp.float32) * score_scale
    grad_keys = dot_first(grad_scores, queries) * score_scale
    grad_values = dot_first(soft_weights.astype(jnp.bfloat16), upstream)
    return (grad_query, jnp.concatenate([grad_keys, grad_values], axis=1))


def shards(
    stream,
    memory,
    cotangent,
    deal_order,
    offsets,
    context_mask,
    w_qkv,
    w_out,
    w_cq,
    w_ckv,
    w_cout,
    w_up,
    w_down,
    b_up,
    gains,
    biases,
):
    tokens = stream[0, 0]
    row_count, model_width = tokens.shape
    head_width = model_width // HEADS
    deal_ids = deal_order[0, 0]
    prompt_blocks = context_mask.shape[3]
    own_blocks = row_count // BLK
    own_ids = lax.dynamic_slice_in_dim(deal_ids, lax.axis_index("ctx") * own_blocks, own_blocks)
    query_pos = (
        own_ids[:, None] * jnp.int32(BLK) + jnp.arange(BLK, dtype=jnp.int32)[None, :]
    ).reshape(-1)
    allowed = visible(
        query_pos, deal_ids, offsets[0, 0], context_mask[0, 0], BLK, prompt_blocks, CBLK
    )
    zeros_row = jnp.zeros((model_width,), jnp.float32)
    projected = (
        jnp.dot(tokens, w_qkv, preferred_element_type=jnp.float32)
        + jnp.concatenate([biases[0], zeros_row, biases[1]])
    ).astype(jnp.bfloat16)
    query_heads = to_heads(projected[:, :model_width], HEADS)
    keyval_own = pair_heads(
        projected[:, model_width : 2 * model_width], projected[:, 2 * model_width :], HEADS
    )
    keyval_all = lax.all_gather(keyval_own, "ctx", axis=1, tiled=True)

    def self_forward(pieces):
        return head_forward(pieces[0], pieces[1], allowed)

    self_out, self_lse = lax.map(self_forward, (query_heads, keyval_all))
    attended = from_heads(self_out).astype(jnp.bfloat16)
    first_sum = (
        tokens.astype(jnp.float32)
        + jnp.dot(attended, w_out, preferred_element_type=jnp.float32)
        + biases[2]
    )
    normed_one = norm_rows(first_sum, gains[0], biases[3])
    normed_low = normed_one.astype(jnp.bfloat16)
    cross_query = (
        jnp.dot(normed_low, w_cq, preferred_element_type=jnp.float32) + biases[4]
    ).astype(jnp.bfloat16)
    cross_bias = jnp.concatenate([zeros_row, biases[5]])
    memory_own = memory[0, 0]
    memory_all = lax.all_gather(memory_own, "ctx", axis=0, tiled=True)
    cross_kv = (jnp.dot(memory_all, w_ckv, preferred_element_type=jnp.float32) + cross_bias).astype(
        jnp.bfloat16
    )
    cross_heads = pair_heads(cross_kv[:, :model_width], cross_kv[:, model_width:], HEADS)
    cross_query_heads = to_heads(cross_query, HEADS)

    def cross_forward(pieces):
        return head_forward(pieces[0], pieces[1], None)

    cross_out, cross_lse = lax.map(cross_forward, (cross_query_heads, cross_heads))
    cross_attended = from_heads(cross_out).astype(jnp.bfloat16)
    second_sum = (
        normed_one + jnp.dot(cross_attended, w_cout, preferred_element_type=jnp.float32) + biases[6]
    )
    normed_two = norm_rows(second_sum, gains[1], biases[7])
    normed_two_low = normed_two.astype(jnp.bfloat16)
    hidden_pre = jnp.dot(normed_two_low, w_up, preferred_element_type=jnp.float32) + b_up
    hidden = gelu_exact(hidden_pre).astype(jnp.bfloat16)
    third_sum = normed_two + jnp.dot(hidden, w_down, preferred_element_type=jnp.float32) + biases[8]
    output = norm_rows(third_sum, gains[2], biases[9])
    grad_third, grad_gain_three, grad_shift_three = norm_back(
        third_sum, gains[2], biases[9], cotangent[0, 0].astype(jnp.float32)
    )
    grad_down_in = grad_third.astype(jnp.bfloat16)
    grad_w_down = dot_first(hidden, grad_down_in)
    grad_b_down = jnp.sum(grad_down_in.astype(jnp.float32), axis=0)
    grad_hidden = dot_last(grad_down_in, w_down)
    _, gelu_pull = jax.vjp(gelu_exact, hidden_pre)
    grad_pre = gelu_pull(grad_hidden)[0].astype(jnp.bfloat16)
    grad_w_up = dot_first(normed_two_low, grad_pre)
    grad_b_up = jnp.sum(grad_pre.astype(jnp.float32), axis=0)
    grad_normed_two = grad_third + dot_last(grad_pre, w_up)
    grad_second, grad_gain_two, grad_shift_two = norm_back(
        second_sum, gains[1], biases[7], grad_normed_two
    )
    grad_cross_in = grad_second.astype(jnp.bfloat16)
    grad_w_cout = dot_first(cross_attended, grad_cross_in)
    grad_b_co = jnp.sum(grad_cross_in.astype(jnp.float32), axis=0)
    grad_cross_heads = to_heads(dot_last(grad_cross_in, w_cout).astype(jnp.bfloat16), HEADS)

    def cross_backward(pieces):
        return head_backward(pieces[0], pieces[1], pieces[2], pieces[3], None)

    grad_cq_heads, grad_ckv_all = lax.map(
        cross_backward, (cross_query_heads, cross_heads, grad_cross_heads, cross_lse)
    )
    grad_ckv_own = lax.psum_scatter(
        grad_ckv_all.astype(jnp.bfloat16), "ctx", scatter_dimension=1, tiled=True
    )
    grad_cv = from_heads(grad_ckv_own[:, :, head_width:])
    grad_ckv = jnp.concatenate([from_heads(grad_ckv_own[:, :, :head_width]), grad_cv], axis=1)
    grad_w_ckv = dot_first(memory_own, grad_ckv)
    grad_b_cv = jnp.sum(grad_cv.astype(jnp.float32), axis=0)
    grad_memory = dot_last(grad_ckv, w_ckv)
    grad_cq = from_heads(grad_cq_heads).astype(jnp.bfloat16)
    grad_w_cq = dot_first(normed_low, grad_cq)
    grad_b_cq = jnp.sum(grad_cq.astype(jnp.float32), axis=0)
    grad_normed_one = grad_second + dot_last(grad_cq, w_cq)
    grad_first, grad_gain_one, grad_shift_one = norm_back(
        first_sum, gains[0], biases[3], grad_normed_one
    )
    grad_att_in = grad_first.astype(jnp.bfloat16)
    grad_w_out = dot_first(attended, grad_att_in)
    grad_b_o = jnp.sum(grad_att_in.astype(jnp.float32), axis=0)
    grad_self_heads = to_heads(dot_last(grad_att_in, w_out).astype(jnp.bfloat16), HEADS)

    def self_backward(pieces):
        return head_backward(pieces[0], pieces[1], pieces[2], pieces[3], allowed)

    grad_q_heads, grad_kv_all = lax.map(
        self_backward, (query_heads, keyval_all, grad_self_heads, self_lse)
    )
    grad_kv_own = lax.psum_scatter(
        grad_kv_all.astype(jnp.bfloat16), "ctx", scatter_dimension=1, tiled=True
    )
    grad_values = from_heads(grad_kv_own[:, :, head_width:])
    grad_queries = from_heads(grad_q_heads).astype(jnp.bfloat16)
    grad_proj = jnp.concatenate(
        [grad_queries, from_heads(grad_kv_own[:, :, :head_width]), grad_values], axis=1
    )
    grad_w_qkv = dot_first(tokens, grad_proj)
    grad_b_q = jnp.sum(grad_queries.astype(jnp.float32), axis=0)
    grad_b_v = jnp.sum(grad_values.astype(jnp.float32), axis=0)
    grad_tokens = grad_first + dot_last(grad_proj, w_qkv)
    gain_grads = jnp.stack([grad_gain_one, grad_gain_two, grad_gain_three])
    shift_grads = jnp.stack(
        [
            grad_b_q,
            grad_b_v,
            grad_b_o,
            grad_shift_one,
            grad_b_cq,
            grad_b_cv,
            grad_b_co,
            grad_shift_two,
            grad_b_down,
            grad_shift_three,
        ]
    )
    (
        part_qkv,
        part_out,
        part_cq,
        part_ckv,
        part_cout,
        part_up,
        part_down,
        part_b_up,
        part_gains,
        part_biases,
    ) = (
        lax.psum_scatter(grad_w_qkv, ("ctx", "wsh"), scatter_dimension=0, tiled=True),
        lax.psum_scatter(grad_w_out, ("ctx", "wsh"), scatter_dimension=0, tiled=True),
        lax.psum_scatter(grad_w_cq, ("ctx", "wsh"), scatter_dimension=0, tiled=True),
        lax.psum_scatter(grad_w_ckv, ("ctx", "wsh"), scatter_dimension=0, tiled=True),
        lax.psum_scatter(grad_w_cout, ("ctx", "wsh"), scatter_dimension=0, tiled=True),
        lax.psum_scatter(grad_w_up, ("ctx", "wsh"), scatter_dimension=0, tiled=True),
        lax.psum_scatter(grad_w_down, ("ctx", "wsh"), scatter_dimension=0, tiled=True),
        lax.psum_scatter(grad_b_up, ("ctx", "wsh"), scatter_dimension=0, tiled=True),
        lax.psum_scatter(gain_grads, ("ctx", "wsh"), scatter_dimension=1, tiled=True),
        lax.psum_scatter(shift_grads, ("ctx", "wsh"), scatter_dimension=1, tiled=True),
    )
    (
        total_qkv,
        total_out,
        total_cq,
        total_ckv,
        total_cout,
        total_up,
        total_down,
        total_b_up,
        total_gains,
        total_biases,
    ) = (
        lax.psum(part_qkv.astype(jnp.bfloat16), "grp").astype(jnp.float32),
        lax.psum(part_out.astype(jnp.bfloat16), "grp").astype(jnp.float32),
        lax.psum(part_cq.astype(jnp.bfloat16), "grp").astype(jnp.float32),
        lax.psum(part_ckv.astype(jnp.bfloat16), "grp").astype(jnp.float32),
        lax.psum(part_cout.astype(jnp.bfloat16), "grp").astype(jnp.float32),
        lax.psum(part_up.astype(jnp.bfloat16), "grp").astype(jnp.float32),
        lax.psum(part_down.astype(jnp.bfloat16), "grp").astype(jnp.float32),
        lax.psum(part_b_up.astype(jnp.bfloat16), "grp").astype(jnp.float32),
        lax.psum(part_gains.astype(jnp.bfloat16), "grp").astype(jnp.float32),
        lax.psum(part_biases.astype(jnp.bfloat16), "grp").astype(jnp.float32),
    )
    return (
        output[None, None],
        grad_tokens[None, None],
        grad_memory[None, None],
        total_qkv,
        total_out,
        total_cq,
        total_ckv,
        total_cout,
        total_up,
        total_down,
        total_b_up,
        total_gains,
        total_biases,
    )


def solution(mesh):
    in_specs = (
        P("grp", "wsh", "ctx", None),
        P("grp", "wsh", "ctx", None),
        P("grp", "wsh", "ctx", None),
        P("grp", "wsh", None),
        P("grp", "wsh", None),
        P("grp", "wsh", None, None),
        P(),
        P(),
        P(),
        P(),
        P(),
        P(),
        P(),
        P(),
        P(),
        P(),
    )
    out_specs = (
        P("grp", "wsh", "ctx", None),
        P("grp", "wsh", "ctx", None),
        P("grp", "wsh", "ctx", None),
        P(("ctx", "wsh"), None),
        P(("ctx", "wsh"), None),
        P(("ctx", "wsh"), None),
        P(("ctx", "wsh"), None),
        P(("ctx", "wsh"), None),
        P(("ctx", "wsh"), None),
        P(("ctx", "wsh"), None),
        P(("ctx", "wsh")),
        P(None, ("ctx", "wsh")),
        P(None, ("ctx", "wsh")),
    )
    return jax.shard_map(shards, mesh=mesh, in_specs=in_specs, out_specs=out_specs, check_vma=False)
```

profile of v0, /device:TPU:0, one launch (start us, length us, event | category | flops | bytes accessed | tf_op | source)
XLA Modules:
  0.0 1475.2 jit_solution(13454079716857460875)
XLA Ops:
  19.6 33.4 %all-gather.6.cloned.1.call-done = bf16[1,1,1024,512]{3,2,1,0:T(8,128)(2,1)} async-done(((bf16[1,1,128,512]{3,2,1,0:T(8,128)(2,1)}), bf16[1,1,1024,512]{3,2,1,0:T(8,128)(2,1)}) %all-gather.6.cloned.1.call-update) | async-done | bytes 1048592 | tf_op jit(solution)/shard_map/all_gather | solution.py:184
  53.0 2.8 add_convert_fusion
  57.0 2.8 copy.75
  61.6 5.0 pad_maximum_fusion
  66.6 87.8 %all-gather.4.cloned.1.call-done = bf16[8,3072,128]{1,2,0:T(8,128)(2,1)} async-done(((bf16[8,384,128]{1,2,0:T(8,128)(2,1)}), bf16[8,3072,128]{1,2,0:T(8,128)(2,1)}) %all-gather.4.cloned.1.call-update) | async-done | bytes 6291472 | tf_op jit(solution)/shard_map/all_gather | solution.py:165
  154.4 8.7 copy.71
  163.1 71.3 %while.52 = (s32[]{:T(128)}, bf16[8,384,64]{1,2,0:T(8,128)(2,1)S(1)}, f32[8,384,1]{1,2,0:T(1,128)S(1)}, bf16[8,384,64]{2,1,0:T(8,128)(2,1)}, bf16[8,3072,128]{2,...) while((s32[]{:T(128)}, ...), condition=%wide.region_3.4_spmd.clone, body=%wide.region_0.3_spmd.clone.sunk | while | flops 322043520 | bytes 19919396 | solution.py:170
  166.0 3.7 fusion.229
  174.9 3.7 fusion.229
  183.8 3.7 fusion.229
  192.8 3.7 fusion.229
  201.7 3.7 fusion.229
  210.6 3.7 fusion.229
  219.5 3.7 fusion.229
  228.4 3.7 fusion.229
  242.9 27.4 %while.50 = (s32[]{:T(128)}, bf16[8,384,64]{1,2,0:T(8,128)(2,1)S(1)}, f32[8,384,1]{1,2,0:T(1,128)S(1)}, bf16[8,384,64]{2,1,0:T(8,128)(2,1)}, bf16[8,1024,128]{2,1,0:T(8,128)(2,1)}, /*index=5*/s32[]{:T(128)}) while((s32[]{:T(128)}, bf16[8,384,64]{1,2,0:T(8,128)(2,1)S(1)}, f32[8,384,1]{1,2,0:T(1,128)S(1)}, bf16[8,384,64]{2,1,0:T(8,128)(2,1)}, ...), condition=%wide.region_9.10_spmd, body=%wide.region_6.9_spmd.sunk | while | flops 103415424 | bytes 5980765 | solution.py:194
  272.3 7.4 multiply_convert_fusion.2
  284.9 12.7 multiply_reduce_fusion.2
  300.1 59.7 %while.51 = (s32[]{:T(128)}, bf16[8,384,64]{1,2,0:T(8,128)(2,1)S(1)}, bf16[8,1024,128]{1,2,0:T(8,128)(2,1)}, bf16[8,384,64]{2,1,0:T(8,128)(2,1)}, bf16[8,1024,12...) while((s32[]{:T(128)}, ...), condition=%wide.region_20.21_spmd, body=%wide.region_18.20_spmd.sunk | while | flops 255483520 | bytes 14294653 | solution.py:228
  359.8 3.4 copy.89
  369.9 123.8 %while.53 = (s32[]{:T(128)}, bf16[8,384,64]{1,2,0:T(8,128)(2,1)}, bf16[8,3072,128]{1,2,0:T(8,128)(2,1)}, bf16[8,384,64]{2,1,0:T(8,128)(2,1)}, bf16[8,3072,128]{2...) while((s32[]{:T(128)}, bf16[8,384,64]{1,2,0:T(8,128)(2,1)}, ...), condition=%wide.region_25.26_spmd.clone, body=%wide.region_23.25_spmd.clone.sunk | while | flops 778198656 | bytes 44486212 | solution.py:254
  374.5 4.4 multiply_reduce_fusion.12
  390.0 4.4 multiply_reduce_fusion.12
  405.4 4.4 multiply_reduce_fusion.12
  420.9 4.4 multiply_reduce_fusion.12
  436.4 4.4 multiply_reduce_fusion.12
  451.9 4.4 multiply_reduce_fusion.12
  467.4 4.4 multiply_reduce_fusion.12
  482.8 4.4 multiply_reduce_fusion.12
  493.7 9.0 copy.87
  502.6 7.1 copy.117
  517.9 108.1 %reduce-scatter.34.cloned.1.call-done = bf16[384,1024]{1,0:T(8,128)(2,1)} async-done(((bf16[3072,1024]{1,0:T(8,128)(2,1)}), bf16[384,1024]{1,0:T(8,128)(2,1)}) %reduce-scatter.34.cloned.1.call-update) | async-done | bytes 786448
  631.4 4.7 fusion.117
  637.6 3.3 fusion.142
  647.9 3.6 copy.91
  653.4 40.6 %all-reduce.1 = bf16[2048]{0:T(1024)(128)(2,1)S(1)} all-reduce(f32[2048]{0:T(1024)S(1)} %get-tuple-element.506), channel_id=12, replica_groups=mesh['grp'=2,'ctx'=8,'wsh'=2] {'ctx','wsh'}, use_global_device_ids=true, to_apply=%region_43.44.clone | all-reduce | flops 2048 | bytes 12288
  694.6 9.4 reduce-scatter.42.cloned.1.call-done
  705.3 74.9 %reduce-scatter.26.cloned.1.call-done = f32[32,512]{1,0:T(8,128)} async-done(((f32[512,512]{1,0:T(8,128)}), f32[32,512]{1,0:T(8,128)}) %reduce-scatter.26.cloned.1.call-update) | async-done | bytes 65552 | tf_op jit(solution)/shard_map/reduce_scatter | solution.py:298
  781.7 75.1 %reduce-scatter.28.cloned.1.call-done = f32[32,512]{1,0:T(8,128)} async-done(((f32[512,512]{1,0:T(8,128)}), f32[32,512]{1,0:T(8,128)}) %reduce-scatter.28.cloned.1.call-update) | async-done | bytes 65552 | tf_op jit(solution)/shard_map/reduce_scatter | solution.py:300
  858.2 75.0 %reduce-scatter.24.cloned.1.call-done = f32[32,512]{1,0:T(8,128)} async-done(((f32[512,512]{1,0:T(8,128)}), f32[32,512]{1,0:T(8,128)}) %reduce-scatter.24.cloned.1.call-update) | async-done | bytes 65552 | tf_op jit(solution)/shard_map/reduce_scatter | solution.py:297
  934.7 74.0 %reduce-scatter.44.cloned.1.call-done = f32[32,10]{1,0:T(8,128)} async-done(((f32[512,10]{1,0:T(8,128)}), f32[32,10]{1,0:T(8,128)}) %reduce-scatter.44.cloned.1.call-update) | async-done | bytes 1296
  1010.2 92.2 %reduce-scatter.30.cloned.1.call-done = f32[32,2048]{1,0:T(8,128)} async-done(((f32[512,2048]{1,0:T(8,128)}), f32[32,2048]{1,0:T(8,128)}) %reduce-scatter.30.cloned.1.call-update) | async-done | bytes 262160 | tf_op jit(solution)/shard_map/reduce_scatter | solution.py:301
  1104.1 95.5 %reduce-scatter.32.cloned.1.call-done = f32[128,512]{1,0:T(8,128)} async-done(((f32[2048,512]{1,0:T(8,128)}), f32[128,512]{1,0:T(8,128)}) %reduce-scatter.32.cloned.1.call-update) | async-done | bytes 262160 | tf_op jit(solution)/shard_map/reduce_scatter | solution.py:302
  1201.2 80.6 %reduce-scatter.40.cloned.1.call-done = f32[32,1024]{1,0:T(8,128)} async-done(((f32[512,1024]{1,0:T(8,128)}), f32[32,1024]{1,0:T(8,128)}) %reduce-scatter.40.cloned.1.call-update) | async-done | bytes 131088
  1283.6 131.9 %reduce-scatter.38.cloned.1.call-done = f32[32,1536]{1,0:T(8,128)} async-done(((f32[512,1536]{1,0:T(8,128)}), f32[32,1536]{1,0:T(8,128)}) %reduce-scatter.38.cloned.1.call-update) | async-done | bytes 196624
  1420.0 3.4 fusion.75
  1423.3 13.7 all-reduce.7.cloned.1.call-done
  1444.8 16.7 %all-reduce.9.cloned.1.call-done = (bf16[32,1536]{0,1:T(8,128)(2,1)}, bf16[32,1024]{0,1:T(8,128)(2,1)}, bf16[32,2048]{1,0:T(8,128)(2,1)}, bf16[128,512]{1,0:T(8,128)(2,1)}) async-done(((bf16[32,1536]{0,1:T(8,128)(2,1)}, bf16[32,1024]{0,1:T(8,128)(2,1)}, bf16[32,2048]{1,0:T(8,128)(2,1)}, bf16[128,512]{1,0:T(8,128)(2,1)}), (bf16[32,1536]{0,1:T(8,128)(2,1)}, bf16[32,1024]{0,1:T(8,128)(2,1)}, ...) | async-done | bytes 426000 | tf_op jit(solution)/shard_map/psum | solution.py:319
  (471 shorter events, 309.4 us)
Async XLA Ops:
  7.2 265.1 %copy-start = (bf16[512,2048]{1,0:T(8,128)(2,1)S(1)}, bf16[512,2048]{1,0:T(8,128)(2,1)}, u32[]{:S(2)}) copy-start(bf16[512,2048]{1,0:T(8,128)(2,1)} %param.35) | copy-start | bytes 6291460
  7.2 45.8 %all-gather.6.cloned.1.call-start = ((), (), s32[]{:S(2)}) async-start(), calls=%async_computation.17 | async-start | bytes 1179648 | tf_op jit(solution)/shard_map/all_gather | solution.py:184
  7.9 146.5 %all-gather.4.cloned.1.call-start = ((), (), s32[]{:S(2)}) async-start(), calls=%async_computation.11 | async-start | bytes 7077888 | tf_op jit(solution)/shard_map/all_gather | solution.py:165
  11.4 4.0 copy-start.32
  11.4 4.0 copy-start.35
  14.6 501.8 %reduce-scatter.36.cloned.1.call-start = ((), (), s32[]{:S(2)}) async-start(), calls=%async_computation.19 | async-start | bytes 2359296
  15.4 4.1 copy-start.31
  234.4 8.4 copy-start.5
  270.3 9.4 copy-start.22
  270.3 2.0 copy-start.34
  272.0 25.7 %copy-start.2 = (f32[384,512]{1,0:T(8,128)}, f32[384,512]{1,0:T(8,128)S(1)}, u32[]{:S(2)}) copy-start(f32[384,512]{1,0:T(8,128)S(1)} %get-tuple-element.557) | copy-start | bytes 2359300
  272.3 7.4 copy-start.33
  279.7 1.2 copy-start.13
  279.7 1.4 copy-start.11
  283.0 1.9 copy-start.18
  284.9 12.7 copy-start.26
  298.0 2.0 copy-start.4
  298.2 1.8 copy-start.7
  365.1 260.9 %reduce-scatter.34.cloned.1.call-start = ((), (), s32[]{:S(2)}) async-start(), calls=%async_computation.18 | async-start | bytes 7077888
  365.1 2.6 copy-start.17
  367.5 2.3 copy-start.15
  367.7 2.1 copy-start.9
  509.7 2.8 copy-start.8
  509.7 2.8 copy-start.23
  509.7 194.2 %reduce-scatter.42.cloned.1.call-start = ((), (), s32[]{:S(2)}) async-start(), calls=%async_computation.22 | async-start | bytes 278528
  510.7 3.4 copy-start.6
  510.7 3.4 copy-start.10
  510.7 269.5 %reduce-scatter.26.cloned.1.call-start = ((), (), s32[]{:S(2)}) async-start(), calls=%async_computation.13 | async-start | bytes 1114112 | tf_op jit(solution)/shard_map/reduce_scatter | solution.py:298
  512.5 3.4 copy-start.12
  512.5 3.7 copy-start.20
  512.5 344.3 %reduce-scatter.28.cloned.1.call-start = ((), (), s32[]{:S(2)}) async-start(), calls=%async_computation.14 | async-start | bytes 1114112 | tf_op jit(solution)/shard_map/reduce_scatter | solution.py:300
  514.0 419.2 %reduce-scatter.24.cloned.1.call-start = ((), (), s32[]{:S(2)}) async-start(), calls=%async_computation.12 | async-start | bytes 1114112 | tf_op jit(solution)/shard_map/reduce_scatter | solution.py:297
  515.5 493.2 %reduce-scatter.44.cloned.1.call-start = ((), (), s32[]{:S(2)}) async-start(), calls=%async_computation.23 | async-start | bytes 278528
  626.0 5.4 copy-start.3
  630.1 1.2 copy-start.24
  631.3 471.1 %reduce-scatter.30.cloned.1.call-start = ((), (), s32[]{:S(2)}) async-start(), calls=%async_computation.15 | async-start | bytes 4456448 | tf_op jit(solution)/shard_map/reduce_scatter | solution.py:301
  636.1 1.4 copy-start.14
  636.1 1.5 copy-start.19
  636.1 563.4 %reduce-scatter.32.cloned.1.call-start = ((), (), s32[]{:S(2)}) async-start(), calls=%async_computation.16 | async-start | bytes 4456448 | tf_op jit(solution)/shard_map/reduce_scatter | solution.py:302
  640.9 641.0 %reduce-scatter.40.cloned.1.call-start = ((), (), s32[]{:S(2)}) async-start(), calls=%async_computation.21 | async-start | bytes 2228224
  642.2 2.5 copy-start.21
  644.0 1.1 copy-start.29
  644.1 771.5 %reduce-scatter.38.cloned.1.call-start = ((), (), s32[]{:S(2)}) async-start(), calls=%async_computation.20 | async-start | bytes 3342336
  644.6 6.9 copy-start.30
  651.5 768.4 %copy-start.16 = (f32[384,512]{1,0:T(8,128)S(1)}, f32[384,512]{1,0:T(8,128)}, u32[]{:S(2)}) copy-start(f32[384,512]{1,0:T(8,128)} %copy-done.15) | copy-start | bytes 2359300
  651.5 785.5 %all-reduce.7.cloned.1.call-start = ((), (), s32[]{:S(2)}) async-start(), calls=%async_computation.24 | async-start | bytes 207872 | tf_op jit(solution)/shard_map/psum | solution.py:320
  1010.1 451.3 %all-reduce.9.cloned.1.call-start = ((), (), s32[]{:S(2)}) async-start(), calls=%async_computation.25 | async-start | bytes 1835008 | tf_op jit(solution)/shard_map/psum | solution.py:319
  1417.4 50.9 %copy-start.1 = (bf16[512,2048]{1,0:T(8,128)(2,1)S(1)}, bf16[512,2048]{1,0:T(8,128)(2,1)}, u32[]{:S(2)}) copy-start(bf16[512,2048]{1,0:T(8,128)(2,1)} %param.35) | copy-start | bytes 6291460
  (4 other events, 3.6 us)
Sparse Core Ops, SparseCore 0:
  10.2 42.8 all-gather.5
  55.7 98.6 all-gather.3
  365.2 65.7 reduce-scatter.35
  509.8 116.1 reduce-scatter.33
  628.7 75.2 reduce-scatter.41
  706.2 73.9 reduce-scatter.25
  782.5 74.2 reduce-scatter.27
  859.1 74.0 reduce-scatter.23
  936.1 72.5 reduce-scatter.43
  1011.0 91.4 reduce-scatter.29
  1104.8 94.7 reduce-scatter.31
  1201.8 79.9 reduce-scatter.39
  1287.6 127.8 reduce-scatter.37
  1419.4 17.5 all-reduce.6
  1440.7 20.7 all-reduce.8
where the time goes:
time: 1490 us; the launch traced here: 1480 us
  waiting for transfers between devices  969 us (65%)
  matrix products  241 us (16%)
  local copies, waits for them, and re-layouts  139 us (9%)
  other arithmetic  66 us (4%)
  blocking collectives  40.6 us (3%)
  between operations  16.4 us (1%)
    unnamed x21, waiting for transfers between devices  405 us
    dot_general x55, matrix products, dot_last(): lax.dot_general(left, right, (((1,), (1,)), ((), ())), preferred_element_...  135 us
    reduce_scatter x1, waiting for transfers between devices, shards(): lax.psum_scatter(grad_w_down, ('ctx', 'wsh'), scatter_dimension=0, tiled=...  95.5 us
    reduce_scatter x1, waiting for transfers between devices, shards(): lax.psum_scatter(grad_w_up, ('ctx', 'wsh'), scatter_dimension=0, tiled=True)  92.2 us
    all_gather x1, waiting for transfers between devices, shards(): keyval_all = lax.all_gather(keyval_own, 'ctx', axis=1, tiled=True)  87.8 us
    reduce_scatter x1, waiting for transfers between devices, shards(): lax.psum_scatter(grad_w_cout, ('ctx', 'wsh'), scatter_dimension=0, tiled=...  75.1 us
    reduce_scatter x1, waiting for transfers between devices, shards(): lax.psum_scatter(grad_w_out, ('ctx', 'wsh'), scatter_dimension=0, tiled=T...  75 us
    reduce_scatter x1, waiting for transfers between devices, shards(): lax.psum_scatter(grad_w_cq, ('ctx', 'wsh'), scatter_dimension=0, tiled=True)  74.9 us
  transfers between devices with their start and end apart: 15, of which 14 were waited for; matrix products, arithmetic and copies ran while one was open for 15% of the time, Pallas kernels for 0%

commit v1 on v0

--- a/solution.py
+++ b/solution.py
@@ -1,6 +1,8 @@
 import jax
 import jax.numpy as jnp
 from jax import lax
+from jax.experimental import pallas as pl
+from jax.experimental.pallas import tpu as pltpu
 from jax.sharding import PartitionSpec as P
 
 HEADS = 8
@@ -10,6 +12,974 @@
 
 NEG_FILL = -1000000000.0
 EPS_NORM = 1e-05
+
+
+MESH_ID = pl.DeviceIdType.MESH
+TILE = 512
+STEP = 256
+BIG_VMEM = 62 << 20
+LOW = jnp.bfloat16
+WIDE = jnp.float32
+SHARDS = 16
+HALF = 16
+ROWS = 4
+PIECES = dict(
+    up0=1024, up1=1024, down0=1024, down1=1024, cross=1024, out=512, ckv=1024, qkv0=768, qkv1=768
+)
+TURNS = dict(up0=0, up1=1, down0=0, down1=1, cross=0, out=1, ckv=1, qkv0=0, qkv1=1)
+FEW_ROWS = 24
+
+
+def nn(left, right):
+    return lax.dot_general(
+        left, right, (((1,), (0,)), ((), ())), preferred_element_type=WIDE
+    )
+
+
+def nt(left, right):
+    return lax.dot_general(
+        left, right, (((1,), (1,)), ((), ())), preferred_element_type=WIDE
+    )
+
+
+def swap(block):
+    return block.astype(WIDE).T.astype(block.dtype)
+
+
+def plus(left, right):
+    return left.astype(WIDE) + right.astype(WIDE)
+
+
+def column_sums(values):
+    return jnp.sum(values.astype(WIDE), axis=0, keepdims=True)
+
+
+def norm_parts(values):
+    center = values - jnp.mean(values, axis=-1, keepdims=True)
+    spread = jnp.mean(center * center, axis=-1, keepdims=True)
+    scale = lax.rsqrt(spread + EPS_NORM)
+    return center * scale, scale
+
+
+def norm_pull(unit, scale, gain, upstream):
+    inner = upstream * gain
+    first = jnp.mean(inner, axis=-1, keepdims=True)
+    second = jnp.mean(inner * unit, axis=-1, keepdims=True)
+    return scale * (inner - first - unit * second)
+
+
+def hide_later(scores):
+    rows = lax.broadcasted_iota(jnp.int32, scores.shape, 0)
+    cols = lax.broadcasted_iota(jnp.int32, scores.shape, 1)
+    return jnp.where(rows <= cols, scores, NEG_FILL)
+
+
+def hide_prompt(scores, lim_ref, tile, chunk, prompt_blocks):
+    span = TILE // BLK
+    rows = lax.broadcasted_iota(jnp.int32, (BLK, BLK), 0)
+    columns = []
+    for q_sub in range(span):
+        pieces = []
+        for k_sub in range(span):
+            key_block = chunk * span + k_sub
+            limit = lim_ref[tile * span + q_sub - prompt_blocks, key_block] - key_block * BLK
+            part = scores[k_sub * BLK : (k_sub + 1) * BLK, q_sub * BLK : (q_sub + 1) * BLK]
+            pieces.append(jnp.where(rows < limit, part, NEG_FILL))
+        columns.append(jnp.concatenate(pieces, axis=0))
+    return jnp.concatenate(columns, axis=1)
+
+
+def apart(upper, lower):
+    none = jnp.zeros_like(upper)
+    return jnp.concatenate(
+        [jnp.concatenate([upper, none], axis=1), jnp.concatenate([none, lower], axis=1)], axis=0
+    )
+
+
+def apart_columns(pair):
+    lanes = lax.broadcasted_iota(jnp.int32, pair.shape, 1)
+    wide = pair.astype(WIDE)
+    left = jnp.where(lanes < pair.shape[1] // 2, wide, 0.0).astype(pair.dtype)
+    right = jnp.where(lanes < pair.shape[1] // 2, 0.0, wide).astype(pair.dtype)
+    return jnp.concatenate([left, right], axis=0)
+
+
+def remote(src_ref, dst_ref, send_sem, recv_sem, target):
+    return pltpu.make_async_remote_copy(
+        src_ref=src_ref,
+        dst_ref=dst_ref,
+        send_sem=send_sem,
+        recv_sem=recv_sem,
+        device_id=target,
+        device_id_type=MESH_ID,
+    )
+
+
+class Bag:
+    def __init__(self, items):
+        self.__dict__.update(items)
+
+
+class Spot:
+    def __init__(self):
+        ctx = lax.axis_index("ctx")
+        self.grp, self.ctx, self.wsh = lax.axis_index("grp"), ctx, lax.axis_index("wsh")
+        self.row, self.col = ctx // 2, lax.rem(ctx, 2)
+        self.core_peer = (1 - self.grp, ctx, self.wsh)
+        self.wsh_peer = (self.grp, ctx, 1 - self.wsh)
+        self.col_peer = self.at_row_col(self.row, 1 - self.col)
+        self.rows_by_step = [lax.rem(self.row + step, ROWS) for step in range(ROWS)]
+        self.row_peers = [self.at_row_col(row, self.col) for row in self.rows_by_step]
+        near = self.row + 1 - 2 * lax.rem(self.row, 2)
+        self.few_peers = [
+            self.core_peer, self.wsh_peer, self.col_peer,
+            self.at_row_col(near, self.col), self.row_peers[2],
+        ]
+        self.ctx_by_step = [lax.rem(ctx + step, HEADS) for step in range(HEADS)]
+        self.ctx_peers = [(self.grp, peer, self.wsh) for peer in self.ctx_by_step]
+
+    def at_row_col(self, row, col):
+        return (self.grp, row * 2 + col, self.wsh)
+
+    def greet(self):
+        barrier = pltpu.get_barrier_semaphore()
+        targets = [self.core_peer, self.wsh_peer] + self.ctx_peers[1:]
+        for target in targets:
+            pl.semaphore_signal(barrier, inc=1, device_id=target, device_id_type=MESH_ID)
+        pl.semaphore_wait(barrier, len(targets))
+
+
+class Exchange:
+    def __init__(self, spot, source, target, sems):
+        self.spot, self.source, self.target, self.sems = spot, source, target, sems
+        self.copies = []
+
+    def start(self):
+        spot, own_blocks = self.spot, self.source.shape[1]
+        here = pl.ds(spot.ctx * own_blocks, own_blocks)
+        for step in range(1, HEADS):
+            copy = remote(
+                self.source.at[spot.ctx_by_step[step]], self.target.at[here],
+                self.sems.at[0, step], self.sems.at[1, step], spot.ctx_peers[step],
+            )
+            copy.start()
+            self.copies.append(copy)
+        self.target[here] = self.source[spot.ctx]
+
+    def wait(self):
+        for copy in self.copies:
+            copy.wait()
+
+
+class Spread:
+    def __init__(self, spot, source, target, sems):
+        self.spot, self.source, self.target, self.sems = spot, source, target, sems
+        self.copies = []
+
+    def start(self):
+        spot = self.spot
+        for step in range(1, HEADS):
+            copy = remote(
+                self.source, self.target.at[spot.ctx],
+                self.sems.at[0, step], self.sems.at[1, step], spot.ctx_peers[step],
+            )
+            copy.start()
+            self.copies.append(copy)
+        self.target[pl.ds(spot.ctx, 1)] = self.source[...][None]
+
+    def wait(self):
+        for copy in self.copies:
+            copy.wait()
+
+
+class Piece:
+    def __init__(self, spot, turn, refs, outs):
+        self.spot, self.turn, self.sems, self.outs = spot, turn, refs.sems, outs
+        self.part, self.core_land, self.hop_land = refs.part, refs.core_land, refs.hop_land
+        self.turn_land, self.row_land = refs.turn_land, refs.row_land
+        self.turn_sum = self.core_land.at[:, 0]
+        self.copies = []
+        self.stage = 0
+
+    def copy(self, index, source, target_ref, target):
+        copy = remote(source, target_ref, self.sems.at[0, index], self.sems.at[1, index], target)
+        copy.start()
+        self.copies.append(copy)
+
+    def finish(self):
+        for copy in self.copies:
+            copy.wait()
+        self.copies = []
+
+    def step(self):
+        spot, part = self.spot, self.part
+        own = spot.grp
+        if self.stage == 0:
+            self.copy(0, part.at[1 - own], self.core_land, spot.core_peer)
+        elif self.stage == 1:
+            self.finish()
+            part[own] = plus(part[own], self.core_land[...]).astype(LOW)
+            if self.turn == 0:
+                self.copy(1, part.at[own, :, :, 1 - spot.wsh], self.hop_land, spot.wsh_peer)
+            else:
+                self.copy(1, part.at[own, :, 1 - spot.col], self.hop_land, spot.col_peer)
+        elif self.stage == 2:
+            self.finish()
+            if self.turn == 0:
+                mine = part[own, :, :, spot.wsh]
+                away, target = 1 - spot.col, spot.col_peer
+            else:
+                mine = part[own, :, spot.col]
+                away, target = 1 - spot.wsh, spot.wsh_peer
+            self.turn_sum[...] = plus(mine, self.hop_land[...]).astype(LOW)
+            self.copy(2, self.turn_sum.at[:, away], self.turn_land, target)
+        elif self.stage == 3:
+            self.finish()
+            keep = spot.col if self.turn == 0 else spot.wsh
+            self.turn_land[...] = plus(self.turn_sum[:, keep], self.turn_land[...]).astype(LOW)
+            for step in range(1, ROWS):
+                self.copy(
+                    2 + step, self.turn_land.at[spot.rows_by_step[step]],
+                    self.row_land.at[step - 1], spot.row_peers[step],
+                )
+        elif self.stage == 4:
+            self.finish()
+            total = self.turn_land[spot.row].astype(WIDE)
+            for step in range(ROWS - 1):
+                total = total + self.row_land[step].astype(WIDE)
+            at = 0
+            for index, (out_ref, row, column, width) in enumerate(self.outs):
+                here = (
+                    pl.ds(pl.multiple_of(row + own * HALF, HALF), HALF),
+                    slice(column, column + width),
+                )
+                out_ref[here] = total[:, at : at + width]
+                at += width
+                self.copy(6 + index, out_ref.at[here], out_ref.at[here], spot.core_peer)
+        elif self.stage == 5:
+            self.finish()
+        self.stage += 1
+
+
+def layer_kernel(
+    prompt_blocks,
+    inv_ref, deal_ref, lim_ref, tokens_ref, memory_ref, cot_ref,
+    w_qkv_hbm, w_out_hbm, w_cq_hbm, w_ckv_hbm, w_cout_hbm, w_up_hbm, w_down_hbm,
+    b_up_ref, gains_ref, biases_ref,
+    output_ref, g_stream_ref, g_memory_ref, o_qkv_ref, o_out_ref, o_cq_ref, o_ckv_ref, o_cout_ref,
+    o_up_ref, o_down_ref, few_out_ref,
+    refs,
+):
+    spot = Spot()
+    row_count, width = tokens_ref.shape
+    own_blocks = row_count // BLK
+    head = width // HEADS
+    blocks = own_blocks * HEADS
+    mem_rows = memory_ref.shape[0]
+    mem_total = mem_rows * HEADS
+    hidden_width = b_up_ref.shape[1]
+    chunks = hidden_width // width
+    pairs = HEADS // 2
+    score_scale = head ** (-0.5)
+    prompt_tiles = prompt_blocks * BLK // TILE
+    tiles = blocks * BLK // TILE
+
+    sources = dict(
+        w_qkv=w_qkv_hbm, w_ckv=w_ckv_hbm, w_out=w_out_hbm, w_cq=w_cq_hbm, w_cout=w_cout_hbm,
+        w_up=w_up_hbm, w_down=w_down_hbm,
+    )
+    loads = Bag(
+        {
+            name: pltpu.make_async_copy(source, getattr(refs, name), refs.load_sem.at[index])
+            for index, (name, source) in enumerate(sources.items())
+        }
+    )
+    for name in sources:
+        getattr(loads, name).start()
+
+    outs = dict(
+        up0=[(o_up_ref, 0, 0, 1024)],
+        up1=[(o_up_ref, 0, 1024, 1024)],
+        down0=[(o_down_ref, 0, 0, 512), (o_down_ref, 32, 0, 512)],
+        down1=[(o_down_ref, 64, 0, 512), (o_down_ref, 96, 0, 512)],
+        cross=[(o_cout_ref, 0, 0, 512), (o_cq_ref, 0, 0, 512)],
+        out=[(o_out_ref, 0, 0, 512)],
+        ckv=[(o_ckv_ref, 0, 0, 1024)],
+        qkv0=[(o_qkv_ref, 0, 0, 768)],
+        qkv1=[(o_qkv_ref, 0, 768, 768)],
+    )
+    piece = Bag(
+        {
+            name: Piece(spot, TURNS[name], Bag(refs.pieces[name]), outs[name])
+            for name in PIECES
+        }
+    )
+    ups, downs = (piece.up0, piece.up1), (piece.down0, piece.down1)
+
+    def put_rows(to, values, column):
+        span = values.shape[1]
+        split = values.astype(LOW).reshape(ROWS, 2, 2, 2, HALF, span)
+        for half in range(2):
+            to.part[half, :, :, :, :, column : column + span] = split[:, :, :, half]
+
+    few_ref = refs.few_sum
+    few_ref[0] = jnp.zeros_like(few_ref[0])
+
+    def few(row, values):
+        few_ref[0, row : row + 1, :] = values
+
+    def gain(row):
+        return gains_ref[row : row + 1, :]
+
+    def bias(row):
+        return biases_ref[row : row + 1, :]
+
+    send_ref = refs.head_send
+    loads.w_qkv.wait()
+    zeros_row = jnp.zeros((1, width), WIDE)
+    projected_bias = jnp.concatenate([bias(0), zeros_row, bias(1)], axis=1)
+    for block in range(own_blocks):
+        rows = slice(block * BLK, (block + 1) * BLK)
+        projected = (nn(tokens_ref[rows, :], refs.w_qkv[...]) + projected_bias).astype(LOW)
+        turned = projected.astype(WIDE).T
+        turned = jnp.concatenate([turned[:width] * score_scale, turned[width:]], axis=0).astype(LOW)
+        for h in range(HEADS):
+            for kind in range(3):
+                at = kind * width + h * head
+                send_ref[h, block, kind * head : (kind + 1) * head, :] = turned[at : at + head]
+    spot.greet()
+    to_heads_copy = Exchange(spot, send_ref, refs.head_land, refs.to_heads_sem)
+    to_heads_copy.start()
+    to_heads_copy.wait()
+    spread = Spread(spot, memory_ref, refs.memory_all, refs.spread_sem)
+    spread.start()
+
+    q_ref, kv_ref = refs.q, refs.kv
+    no_head = jnp.zeros((head, BLK), LOW)
+    no_tile = jnp.zeros((head, TILE), LOW)
+    qt_ref, kt_ref, vt_ref = refs.qt, refs.kt, refs.vt
+    exact_ref, lse_ref = refs.exact, refs.lse
+    for pos in range(blocks):
+        block = refs.head_land[inv_ref[pos]]
+        at = slice(pos * BLK, (pos + 1) * BLK)
+        qt_ref[:, at] = block[:head]
+        kt_ref[:, at] = block[head : 2 * head]
+        vt_ref[:, at] = block[2 * head :]
+        q_ref[at, :] = swap(jnp.concatenate([block[:head], no_head], axis=0))
+        kv_ref[at, :] = swap(block[head:])
+
+    def tile_spans(tile, chunk_step, state):
+        state = chunk_step(tile, state, lambda s, c: hide_later(s))
+        first = jnp.where(tile >= prompt_tiles, prompt_tiles, 0)
+        state = lax.fori_loop(first, tile, lambda c, s: chunk_step(c, s, lambda x, _: x), state)
+        return lax.fori_loop(
+            0,
+            first,
+            lambda c, s: chunk_step(
+                c, s, lambda x, cc: hide_prompt(x, lim_ref, tile, cc, prompt_blocks)
+            ),
+            state,
+        )
+
+    def forward_tile(tile, carry):
+        here = pl.ds(pl.multiple_of(tile * TILE, TILE), TILE)
+        queries = jnp.concatenate([qt_ref[:, here], no_tile], axis=0)
+
+        def chunk_step(chunk, state, hide):
+            top, total, mixed = state
+            there = pl.ds(pl.multiple_of(chunk * TILE, TILE), TILE)
+            scores = hide(nn(kv_ref[there, :], queries), chunk)
+            new_top = jnp.maximum(top, jnp.max(scores, axis=0, keepdims=True))
+            weights = jnp.exp(scores - new_top)
+            fade = jnp.exp(top - new_top)
+            total = total * fade + jnp.sum(weights, axis=0, keepdims=True)
+            mixed = mixed * fade + nn(vt_ref[:, there], weights.astype(LOW))
+            return new_top, total, mixed
+
+        top, total, mixed = tile_spans(
+            tile,
+            chunk_step,
+            (
+                jnp.full((1, TILE), NEG_FILL, WIDE),
+                jnp.zeros((1, TILE), WIDE),
+                jnp.zeros((head, TILE), WIDE),
+            ),
+        )
+        exact = mixed / total
+        for sub in range(TILE // BLK):
+            exact_ref[tile * (TILE // BLK) + sub] = exact[:, sub * BLK : (sub + 1) * BLK]
+        lse_ref[:, here] = top + jnp.log(total)
+        return carry
+
+    lax.fori_loop(0, tiles, forward_tile, 0)
+    mixed_ref = refs.mixed_send
+    for row in range(blocks):
+        mixed_ref[row // own_blocks, row % own_blocks] = exact_ref[deal_ref[row]].astype(LOW)
+    from_heads_copy = Exchange(spot, mixed_ref, refs.mixed_land, refs.from_heads_sem)
+    from_heads_copy.start()
+
+    ck_ref, cv_ref, ckt_ref, cvt_ref = refs.ck, refs.cv, refs.ckt, refs.cvt
+    loads.w_ckv.wait()
+    spread.wait()
+    for part in range(HEADS):
+        rows = slice(part * mem_rows, (part + 1) * mem_rows)
+        both = nn(refs.memory_all[part], refs.w_ckv[...])
+        keys = both[:, :width].astype(LOW)
+        values = (both[:, width:] + bias(5)).astype(LOW)
+        ck_ref[rows, :] = keys
+        cv_ref[rows, :] = values
+        ckt_ref[:, rows] = swap(keys)
+        cvt_ref[:, rows] = swap(values)
+
+    loads.w_out.wait()
+    from_heads_copy.wait()
+    attended_t_ref = refs.attended_t
+    unit_one_ref, unit_two_ref = refs.unit_one, refs.unit_two
+    low_one_ref, low_two_ref = refs.low_one, refs.low_two
+    for block in range(own_blocks):
+        at = slice(block * BLK, (block + 1) * BLK)
+        for h in range(HEADS):
+            attended_t_ref[h * head : (h + 1) * head, at] = refs.mixed_land[h * own_blocks + block]
+    cq_ref, cqt_ref = refs.cq, refs.cqt
+    loads.w_cq.wait()
+
+    def rows_at(block):
+        return pl.ds(pl.multiple_of(block * BLK, BLK), BLK)
+
+    def first_norm(block, carry):
+        rows = rows_at(block)
+        attended = swap(attended_t_ref[:, rows])
+        first_sum = tokens_ref[rows, :].astype(WIDE) + nn(attended, refs.w_out[...]) + bias(2)
+        unit, scale = norm_parts(first_sum)
+        unit_one_ref[rows, :] = unit
+        refs.scale_one[rows, :] = scale
+        low_one = (unit * gain(0) + bias(3)).astype(LOW)
+        low_one_ref[rows, :] = low_one
+        cross_query = (nn(low_one, refs.w_cq[...]) + bias(4)).astype(LOW).astype(WIDE)
+        cross_query = cross_query * score_scale
+        cq_ref[rows, :] = cross_query.astype(LOW)
+        cqt_ref[:, rows] = cross_query.T.astype(LOW)
+        return carry
+
+    lax.fori_loop(0, own_blocks, first_norm, 0)
+
+    pair_width = 2 * head
+    scores_ref, weights_ref = refs.scores, refs.weights
+    cross_exact_ref, cross_lse_ref = refs.cross_exact, refs.cross_lse
+    steps = mem_total // STEP
+
+    def pair_at(pair):
+        return pl.ds(pl.multiple_of(pair * pair_width, pair_width), pair_width)
+
+    def step_at(step):
+        return pl.ds(pl.multiple_of(step * STEP, STEP), STEP)
+
+    def cross_forward(pair, carry):
+        lanes = pair_at(pair)
+        for side in range(2):
+            at = pl.ds(pl.multiple_of(pair * pair_width + side * head, head), head)
+            queries = cqt_ref[at, :]
+            none = jnp.zeros_like(queries)
+            queries = jnp.concatenate([none, queries] if side else [queries, none], axis=0)
+
+            def first_pass(step, top):
+                scores = nn(ck_ref[step_at(step), lanes], queries)
+                scores_ref[step_at(step), :] = scores
+                return jnp.maximum(top, jnp.max(scores, axis=0, keepdims=True))
+
+            top = lax.fori_loop(
+                0, steps, first_pass, jnp.full((1, row_count), NEG_FILL, WIDE), unroll=True
+            )
+
+            def second_pass(step, total):
+                weights = jnp.exp(scores_ref[step_at(step), :] - top)
+                weights_ref[step_at(step), :] = weights.astype(LOW)
+                return total + jnp.sum(weights, axis=0, keepdims=True)
+
+            total = lax.fori_loop(
+                0, steps, second_pass, jnp.zeros((1, row_count), WIDE), unroll=True
+            )
+            across = slice(side * row_count, (side + 1) * row_count)
+            cross_lse_ref[pl.ds(pair, 1), across] = top + jnp.log(total)
+            cross_exact_ref[at, :] = nn(cvt_ref[at, :], weights_ref[...]) / total
+        return carry
+
+    lax.fori_loop(0, pairs, cross_forward, 0)
+    cross_low_ref = refs.cross_low
+    total_ref, hidden_ref, slope_ref = g_stream_ref, refs.hidden, refs.slope
+    loads.w_cout.wait()
+
+    def second_norm(block, carry):
+        rows = rows_at(block)
+        cross_low = cross_exact_ref[:, rows].T.astype(LOW)
+        cross_low_ref[rows, :] = cross_low
+        normed_one = unit_one_ref[rows, :] * gain(0) + bias(3)
+        unit, scale = norm_parts(normed_one + nn(cross_low, refs.w_cout[...]) + bias(6))
+        unit_two_ref[rows, :] = unit
+        refs.scale_two[rows, :] = scale
+        normed_two = unit * gain(1) + bias(7)
+        low_two_ref[rows, :] = normed_two.astype(LOW)
+        total_ref[rows, :] = normed_two + bias(8)
+        return carry
+
+    lax.fori_loop(0, own_blocks, second_norm, 0)
+
+    loads.w_up.wait()
+    loads.w_down.wait()
+    w_up_ref, w_down_ref = refs.w_up, refs.w_down
+
+    def chunk_at(chunk):
+        return pl.ds(pl.multiple_of(chunk * width, width), width)
+
+    def up_step(chunk, carry):
+        pre = nn(low_two_ref[...], w_up_ref[:, chunk_at(chunk)]) + b_up_ref[:, chunk_at(chunk)]
+        normal = 0.5 + 0.5 * lax.erf(pre * (2.0**-0.5))
+        hidden = (pre * normal).astype(LOW)
+        hidden_ref[chunk] = hidden
+        slope = normal + pre * jnp.exp(-0.5 * pre * pre) * ((2.0 * jnp.pi) ** -0.5)
+        slope_ref[chunk] = slope.astype(LOW)
+        total_ref[...] += nn(hidden, w_down_ref[chunk_at(chunk), :])
+        return carry
+
+    lax.fori_loop(0, chunks, up_step, 0)
+
+    low_third_ref = refs.low_third
+    no_sums = (zeros_row, zeros_row, zeros_row)
+
+    def third_norm(block, sums):
+        rows = rows_at(block)
+        unit, scale = norm_parts(total_ref[rows, :])
+        output_ref[rows, :] = unit * gain(2) + bias(9)
+        upstream = cot_ref[rows, :].astype(WIDE)
+        grad = norm_pull(unit, scale, gain(2), upstream)
+        low = grad.astype(LOW)
+        low_third_ref[rows, :] = low
+        total_ref[rows, :] = grad
+        return (
+            sums[0] + column_sums(upstream * unit),
+            sums[1] + column_sums(upstream),
+            sums[2] + column_sums(low),
+        )
+
+    sums = lax.fori_loop(0, own_blocks, third_norm, no_sums)
+    few(6, sums[0])
+    few(16, sums[1])
+    few(15, sums[2])
+
+    turned_ref = refs.turned
+    turned_ref[...] = swap(low_two_ref[...])
+    for chunk in range(chunks):
+        rows = slice(chunk * width, (chunk + 1) * width)
+        grad_hidden = nt(low_third_ref[...], w_down_ref[rows, :])
+        grad_pre = (grad_hidden * slope_ref[chunk].astype(WIDE)).astype(LOW)
+        few(chunk, column_sums(grad_pre))
+        total_ref[...] += nt(grad_pre, w_up_ref[:, rows])
+        grad_up = nn(turned_ref[...], grad_pre)
+        put_rows(ups[chunk // 2], grad_up, (chunk % 2) * width)
+        if chunk % 2 == 1:
+            ups[chunk // 2].step()
+        grad_down = nn(swap(hidden_ref[chunk]), low_third_ref[...])
+        split = grad_down.astype(LOW).reshape(2, 2, 4, 2, HALF, width)
+        for part in range(4):
+            to = downs[part // 2].part
+            column = (part % 2) * width
+            for half in range(2):
+                to[half, chunk, :, :, :, column : column + width] = split[:, :, part, half]
+    piece.down0.step()
+    piece.down1.step()
+
+    dco_ref, dcot_ref = refs.dco, refs.dcot
+
+    def second_back(block, sums):
+        rows = rows_at(block)
+        upstream = total_ref[rows, :]
+        unit = unit_two_ref[rows, :]
+        grad = norm_pull(unit, refs.scale_two[rows, :], gain(1), upstream)
+        low = grad.astype(LOW)
+        total_ref[rows, :] = grad
+        low_third_ref[rows, :] = low
+        dco_ref[rows, :] = nt(low, refs.w_cout[...]).astype(LOW)
+        dcot_ref[:, rows] = nt(refs.w_cout[...], low).astype(LOW)
+        return (
+            sums[0] + column_sums(upstream * unit),
+            sums[1] + column_sums(upstream),
+            sums[2] + column_sums(low),
+        )
+
+    sums = lax.fori_loop(0, own_blocks, second_back, no_sums)
+    few(5, sums[0])
+    few(14, sums[1])
+    few(13, sums[2])
+    put_rows(piece.cross, nn(swap(cross_low_ref[...]), low_third_ref[...]), 0)
+    piece.up0.step()
+    piece.up1.step()
+
+    dcqt_ref, dsend_ref, dland_ref = refs.dcqt, w_up_ref, refs.dkv_land
+    side_width = ROWS * 2 * pair_width
+    dkv_copies = []
+    for pair in range(pairs):
+        lanes = slice(pair * pair_width, (pair + 1) * pair_width)
+        low_half = slice(pair * pair_width, pair * pair_width + head)
+        high_half = slice(pair * pair_width + head, (pair + 1) * pair_width)
+        queries_t = apart(cqt_ref[low_half, :], cqt_ref[high_half, :])
+        upstream_t = apart(dcot_ref[low_half, :], dcot_ref[high_half, :])
+        queries = apart_columns(cq_ref[:, lanes])
+        upstream = apart_columns(dco_ref[:, lanes])
+        dots = cross_exact_ref[lanes, :] * dcot_ref[lanes, :].astype(WIDE)
+        delta = jnp.concatenate(
+            [column_sums(dots[:head]), column_sums(dots[head:])], axis=1
+        )
+        lse = cross_lse_ref[pair : pair + 1, :]
+        dcqt_ref[lanes, :] = jnp.zeros((pair_width, row_count), WIDE)
+
+        def backward_step(step, carry):
+            there = step_at(step)
+            weights = jnp.exp(nn(ck_ref[there, lanes], queries_t) - lse)
+            grad_weights = nn(cv_ref[there, lanes], upstream_t)
+            grad_scores = (weights * (grad_weights - delta)).astype(LOW)
+            grad_keys = nn(grad_scores, queries).astype(LOW)
+            grad_values = nn(weights.astype(LOW), upstream).astype(LOW)
+            for sub in range(STEP // mem_rows):
+                rows = slice(sub * mem_rows, (sub + 1) * mem_rows)
+                at = sub * side_width + step * 2 * pair_width
+                at = pl.ds(pl.multiple_of(at, pair_width), 2 * pair_width)
+                dsend_ref[pair * mem_rows : (pair + 1) * mem_rows, at] = jnp.concatenate(
+                    [grad_keys[rows], grad_values[rows]], axis=1
+                )
+            dcqt_ref[low_half, :] += nn(ckt_ref[low_half, there], grad_scores[:, :row_count])
+            dcqt_ref[high_half, :] += nn(ckt_ref[high_half, there], grad_scores[:, row_count:])
+            return carry
+
+        lax.fori_loop(0, steps, backward_step, 0)
+        copy = remote(
+            dsend_ref.at[
+                pl.ds(pair * mem_rows, mem_rows),
+                pl.ds(pl.multiple_of((1 - spot.col) * side_width, side_width), side_width),
+            ],
+            dland_ref.at[pair],
+            refs.dkv_sem.at[0, pair], refs.dkv_sem.at[1, pair], spot.col_peer,
+        )
+        copy.start()
+        dkv_copies.append(copy)
+        (downs if pair < 2 else ups)[pair % 2].step()
+
+    upstream_send = refs.mixed_send
+
+    def first_back(block, sums):
+        rows = rows_at(block)
+        grad_cq = (dcqt_ref[:, rows].T * score_scale).astype(LOW)
+        dco_ref[rows, :] = grad_cq
+        upstream = total_ref[rows, :] + nt(grad_cq, refs.w_cq[...])
+        unit = unit_one_ref[rows, :]
+        grad = norm_pull(unit, refs.scale_one[rows, :], gain(0), upstream)
+        low = grad.astype(LOW)
+        total_ref[rows, :] = grad
+        low_third_ref[rows, :] = low
+        grad_attended_t = nt(refs.w_out[...], low).astype(LOW)
+        for h in range(HEADS):
+            upstream_send[h, block] = grad_attended_t[h * head : (h + 1) * head, :]
+        return (
+            sums[0] + column_sums(upstream * unit),
+            sums[1] + column_sums(upstream),
+            sums[2] + column_sums(low),
+            sums[3] + column_sums(grad_cq),
+        )
+
+    sums = lax.fori_loop(0, own_blocks, first_back, no_sums + (zeros_row,))
+    few(4, sums[0])
+    few(10, sums[1])
+    few(9, sums[2])
+    few(11, sums[3])
+    up_heads_copy = Exchange(spot, upstream_send, refs.up_land, refs.up_heads_sem)
+    up_heads_copy.start()
+    turned_ref[...] = swap(low_one_ref[...])
+    put_rows(piece.cross, nn(turned_ref[...], dco_ref[...]), width)
+    piece.cross.step()
+    put_rows(piece.out, nn(attended_t_ref[...], low_third_ref[...]), 0)
+    piece.out.step()
+    piece.down0.step()
+    piece.down1.step()
+    piece.cross.step()
+    up_heads_copy.wait()
+    piece.up0.step()
+    piece.up1.step()
+
+    upq_ref, upt_ref = refs.up, refs.upt
+    dkv_ref, dqt_ref = refs.dkv, refs.dqt
+    for pos in range(blocks):
+        block = refs.up_land[inv_ref[pos]]
+        at = slice(pos * BLK, (pos + 1) * BLK)
+        upt_ref[:, at] = block
+        upq_ref[at, :] = swap(jnp.concatenate([no_head, block], axis=0))
+    dkv_ref[...] = jnp.zeros_like(dkv_ref)
+
+    def backward_tile(tile, carry):
+        here = pl.ds(pl.multiple_of(tile * TILE, TILE), TILE)
+        queries_t = jnp.concatenate([qt_ref[:, here], no_tile], axis=0)
+        upstream_t = jnp.concatenate([no_tile, upt_ref[:, here]], axis=0)
+        both = jnp.concatenate([q_ref[here, :], upq_ref[here, :]], axis=0)
+        lse = lse_ref[:, here]
+        exact = jnp.concatenate(
+            [exact_ref[tile * (TILE // BLK) + sub] for sub in range(TILE // BLK)], axis=1
+        )
+        delta = column_sums(exact * upt_ref[:, here].astype(WIDE))
+
+        def chunk_step(chunk, grad_q, hide):
+            there = pl.ds(pl.multiple_of(chunk * TILE, TILE), TILE)
+            scores = hide(nn(kv_ref[there, :], queries_t), chunk)
+            weights = jnp.exp(scores - lse)
+            grad_weights = nn(kv_ref[there, :], upstream_t)
+            grad_scores = (weights * (grad_weights - delta)).astype(LOW)
+            sides = jnp.concatenate([grad_scores, weights.astype(LOW)], axis=1)
+            spread_at = pl.ds(chunk * (TILE // BLK), TILE // BLK)
+            dkv_ref[spread_at] += nn(sides, both).reshape(TILE // BLK, BLK, 2 * head)
+            return grad_q + nn(kt_ref[:, there], grad_scores)
+
+        grad_q = tile_spans(tile, chunk_step, jnp.zeros((head, TILE), WIDE))
+        grad_q = (grad_q * score_scale).astype(LOW)
+        for sub in range(TILE // BLK):
+            dqt_ref[tile * (TILE // BLK) + sub] = grad_q[:, sub * BLK : (sub + 1) * BLK]
+        return carry
+
+    lax.fori_loop(0, tiles // 2, backward_tile, 0)
+    piece.out.step()
+    piece.cross.step()
+    piece.down0.step()
+    piece.down1.step()
+    dsum_ref, drow_ref = refs.dkv_sum, refs.dkv_row
+    for copy in dkv_copies:
+        copy.wait()
+    own_side = pl.ds(pl.multiple_of(spot.col * side_width, side_width), side_width)
+    for pair in range(pairs):
+        own_rows = slice(pair * mem_rows, (pair + 1) * mem_rows)
+        both = plus(dsend_ref[own_rows, own_side], dland_ref[pair]).astype(LOW)
+        for row in range(ROWS):
+            dsum_ref[row, pair] = both[:, row * 2 * pair_width : (row + 1) * 2 * pair_width]
+    dkv_copies = []
+    for step in range(1, ROWS):
+        copy = remote(
+            dsum_ref.at[spot.rows_by_step[step]], drow_ref.at[step - 1],
+            refs.dkv_sem.at[0, 3 + step], refs.dkv_sem.at[1, 3 + step], spot.row_peers[step],
+        )
+        copy.start()
+        dkv_copies.append(copy)
+    lax.fori_loop(tiles // 2, tiles - 1, backward_tile, 0)
+    piece.out.step()
+    piece.cross.step()
+    lax.fori_loop(tiles - 1, tiles, backward_tile, 0)
+
+    back_send = refs.head_send
+    for row in range(blocks):
+        pos = deal_ref[row]
+        to = (row // own_blocks, row % own_blocks)
+        back_send[to[0], to[1], :head] = dqt_ref[pos]
+        back_send[to[0], to[1], head:] = dkv_ref[pos].T.astype(LOW)
+    back_copy = Exchange(spot, back_send, refs.head_land, refs.back_sem)
+    back_copy.start()
+
+    for copy in dkv_copies:
+        copy.wait()
+    for pair in range(pairs):
+        total = dsum_ref[spot.row, pair].astype(WIDE)
+        for step in range(ROWS - 1):
+            total = total + drow_ref[step, pair].astype(WIDE)
+        refs.dckv[:, pair * pair_width : (pair + 1) * pair_width] = total[:, :pair_width].astype(LOW)
+        at = width + pair * pair_width
+        refs.dckv[:, at : at + pair_width] = total[:, pair_width:].astype(LOW)
+    dckv = refs.dckv[...]
+    put_rows(piece.ckv, nn(swap(memory_ref[...]), dckv), 0)
+    piece.ckv.step()
+    few(12, column_sums(dckv[:, width:]))
+    g_memory_ref[...] = nt(dckv, refs.w_ckv[...])
+    piece.out.step()
+    piece.cross.step()
+    for item in ups + downs:
+        item.step()
+    piece.ckv.step()
+
+    back_copy.wait()
+    for block in range(own_blocks):
+        rows = slice(block * BLK, (block + 1) * BLK)
+        for kind in range(3):
+            turned = jnp.concatenate(
+                [
+                    refs.head_land[h * own_blocks + block, kind * head : (kind + 1) * head, :]
+                    for h in range(HEADS)
+                ],
+                axis=0,
+            )
+            hidden_ref[kind, rows, :] = swap(turned)
+    turned_ref[...] = swap(tokens_ref[...])
+    put_rows(piece.qkv0, nn(turned_ref[...], hidden_ref[0]), 0)
+    grad_keys = nn(turned_ref[...], hidden_ref[1])
+    put_rows(piece.qkv0, grad_keys[:, : width // 2], width)
+    piece.qkv0.step()
+    put_rows(piece.qkv1, grad_keys[:, width // 2 :], 0)
+    put_rows(piece.qkv1, nn(turned_ref[...], hidden_ref[2]), width // 2)
+    piece.qkv1.step()
+    few(7, column_sums(hidden_ref[0]))
+    few(8, column_sums(hidden_ref[2]))
+
+    def few_copy(step):
+        return remote(
+            few_ref.at[step], refs.few_land.at[step],
+            refs.few_sem.at[0, step], refs.few_sem.at[1, step], spot.few_peers[step],
+        )
+
+    few_copy(0).start()
+    piece.ckv.step()
+    grad_stream = total_ref[...]
+    for kind in range(3):
+        lanes = slice(kind * width, (kind + 1) * width)
+        grad_stream = grad_stream + nt(hidden_ref[kind], refs.w_qkv[:, lanes])
+    g_stream_ref[...] = grad_stream
+    piece.qkv0.step()
+    piece.qkv1.step()
+    for step in range(5):
+        few_copy(step).wait()
+        total = few_ref[step] + refs.few_land[step]
+        if step < 4:
+            few_ref[step + 1] = total
+            few_copy(step + 1).start()
+        else:
+            few_out_ref[...] = total
+        if step < 3:
+            piece.qkv0.step()
+            piece.qkv1.step()
+            if step < 2:
+                piece.ckv.step()
+    for name in PIECES:
+        while getattr(piece, name).stage < 6:
+            getattr(piece, name).step()
+
+
+def layer_scratch(row_count, width, hidden_width, mem_rows):
+    own_blocks = row_count // BLK
+    blocks = own_blocks * HEADS
+    head = width // HEADS
+    tokens = blocks * BLK
+    mem_total = mem_rows * HEADS
+    dma = pltpu.SemaphoreType.DMA
+    scratch = dict(
+        w_qkv=((width, 3 * width), LOW), w_ckv=((width, 2 * width), LOW),
+        w_out=((width, width), LOW), w_cq=((width, width), LOW),
+        w_cout=((width, width), LOW), w_up=((width, hidden_width), LOW),
+        w_down=((hidden_width, width), LOW),
+        head_send=((HEADS, own_blocks, 3 * head, BLK), LOW),
+        head_land=((blocks, 3 * head, BLK), LOW),
+        memory_all=((HEADS, mem_rows, width), LOW),
+        q=((tokens, 2 * head), LOW), kv=((tokens, 2 * head), LOW),
+        qt=((head, tokens), LOW), kt=((head, tokens), LOW), vt=((head, tokens), LOW),
+        exact=((blocks, head, BLK), WIDE), lse=((1, tokens), WIDE),
+        mixed_send=((HEADS, own_blocks, head, BLK), LOW),
+        mixed_land=((blocks, head, BLK), LOW),
+        ck=((mem_total, width), LOW), cv=((mem_total, width), LOW),
+        ckt=((width, mem_total), LOW), cvt=((width, mem_total), LOW),
+        attended_t=((width, row_count), LOW),
+        unit_one=((row_count, width), WIDE), unit_two=((row_count, width), WIDE),
+        scale_one=((row_count, 1), WIDE), scale_two=((row_count, 1), WIDE),
+        low_one=((row_count, width), LOW), low_two=((row_count, width), LOW),
+        cq=((row_count, width), LOW), cqt=((width, row_count), LOW),
+        scores=((mem_total, row_count), WIDE), weights=((mem_total, row_count), LOW),
+        cross_exact=((width, row_count), WIDE),
+        cross_lse=((HEADS // 2, 2 * row_count), WIDE),
+        cross_low=((row_count, width), LOW),
+        hidden=((hidden_width // width, row_count, width), LOW),
+        slope=((hidden_width // width, row_count, width), LOW),
+        low_third=((row_count, width), LOW),
+        turned=((width, row_count), LOW),
+        dco=((row_count, width), LOW), dcot=((width, row_count), LOW),
+        dcqt=((width, row_count), WIDE),
+        dkv_land=((HEADS // 2, mem_rows, ROWS * 4 * head), LOW),
+        dkv_sum=((ROWS, HEADS // 2, mem_rows, 4 * head), LOW),
+        dkv_row=((ROWS - 1, HEADS // 2, mem_rows, 4 * head), LOW),
+        dckv=((mem_rows, 2 * width), LOW),
+        up_land=((blocks, head, BLK), LOW),
+        up=((tokens, 2 * head), LOW), upt=((head, tokens), LOW),
+        dkv=((blocks, BLK, 2 * head), WIDE), dqt=((blocks, head, BLK), LOW),
+        few_sum=((5, FEW_ROWS, width), WIDE), few_land=((5, FEW_ROWS, width), WIDE),
+    )
+    out = {name: pltpu.VMEM(shape, kind) for name, (shape, kind) in scratch.items()}
+    out.update(
+        load_sem=dma((7,)), to_heads_sem=dma((2, HEADS)), from_heads_sem=dma((2, HEADS)),
+        up_heads_sem=dma((2, HEADS)), back_sem=dma((2, HEADS)), spread_sem=dma((2, HEADS)),
+        dkv_sem=dma((2, HEADS)), few_sem=dma((2, 5)),
+    )
+    out.update(
+        pieces={
+            name: dict(
+                part=pltpu.VMEM((2, ROWS, 2, 2, HALF, span), LOW),
+                core_land=pltpu.VMEM((ROWS, 2, 2, HALF, span), LOW),
+                hop_land=pltpu.VMEM((ROWS, 2, HALF, span), LOW),
+                turn_land=pltpu.VMEM((ROWS, HALF, span), LOW),
+                row_land=pltpu.VMEM((ROWS - 1, HALF, span), LOW),
+                sems=dma((2, 8)),
+            )
+            for name, span in PIECES.items()
+        }
+    )
+    return out
+
+
+def layer_call(inverse, deal_ids, limits, tokens, memory, cotangent, weights, b_up, gains, biases, prompt_blocks):
+    row_count, width = tokens.shape
+    hidden_width = b_up.shape[1]
+    mem_rows = memory.shape[0]
+    smem = pl.BlockSpec(memory_space=pltpu.SMEM)
+    vmem = pl.BlockSpec(memory_space=pltpu.VMEM)
+    hbm = pl.BlockSpec(memory_space=pl.ANY)
+    scratch = layer_scratch(row_count, width, hidden_width, mem_rows)
+    leaves, tree = jax.tree.flatten(scratch, is_leaf=lambda leaf: not isinstance(leaf, dict))
+    out_shapes = [
+        (row_count, width), (row_count, width), (mem_rows, width),
+        (32, 3 * width), (32, width), (32, width), (32, 2 * width), (32, width),
+        (32, hidden_width), (hidden_width // SHARDS, width), (FEW_ROWS, width),
+    ]
+
+    def body(*args):
+        count = len(args) - len(leaves)
+        refs = Bag(jax.tree.unflatten(tree, args[count:]))
+        layer_kernel(prompt_blocks, *args[:count], refs)
+
+    return pl.pallas_call(
+        body,
+        out_shape=[jax.ShapeDtypeStruct(shape, WIDE) for shape in out_shapes],
+        in_specs=[smem] * 3 + [vmem] * 3 + [hbm] * 7 + [vmem] * 3,
+        out_specs=[vmem] * len(out_shapes),
+        scratch_shapes=leaves,
+        compiler_params=pltpu.CompilerParams(
+            collective_id=0, has_side_effects=True, vmem_limit_bytes=BIG_VMEM
+        ),
+        name="layer",
+    )(inverse, deal_ids, limits, tokens, memory, cotangent, *weights, b_up, gains, biases)
+
+
+def layer_shards(
+    stream, memory, cotangent, deal_order, offsets, context_mask,
+    w_qkv, w_out, w_cq, w_ckv, w_cout, w_up, w_down, b_up, gains, biases,
+):
+    deal_ids = deal_order[0, 0]
+    prompt_blocks = context_mask.shape[3]
+    places = jnp.arange(deal_ids.shape[0], dtype=jnp.int32)
+    inverse = jnp.sum(
+        jnp.where(deal_ids[None, :] == places[:, None], places[None, :], 0), axis=1, dtype=jnp.int32
+    )
+    blocks_open = (context_mask[0, 0] > 0) | (jnp.arange(prompt_blocks)[None, :] == 0)
+    limits = jnp.where(blocks_open, offsets[0, 0, 0], 0).astype(jnp.int32)
+    *grads, few = layer_call(
+        inverse, deal_ids, limits, stream[0, 0], memory[0, 0], cotangent[0, 0],
+        (w_qkv, w_out, w_cq, w_ckv, w_cout, w_up, w_down),
+        b_up[None, :], gains, biases, prompt_blocks,
+    )
+    output, grad_stream, grad_memory = grads[:3]
+    own = lax.axis_index("ctx") * 2 + lax.axis_index("wsh")
+    total_b_up = lax.dynamic_slice_in_dim(few[:4].reshape(-1), own * 128, 128)
+    total_gains = lax.dynamic_slice_in_dim(few[4:7], own * 32, 32, axis=1)
+    total_biases = lax.dynamic_slice_in_dim(few[7:17], own * 32, 32, axis=1)
+    return (
+        output[None, None], grad_stream[None, None], grad_memory[None, None],
+        *grads[3:], total_b_up, total_gains, total_biases,
+    )
 
 
 def gelu_exact(values):
@@ -378,4 +1348,5 @@
         P(None, ("ctx", "wsh")),
         P(None, ("ctx", "wsh")),
     )
-    return jax.shard_map(shards, mesh=mesh, in_specs=in_specs, out_specs=out_specs, check_vma=False)
+    body = layer_shards if mesh.shape["ctx"] == HEADS else shards
+    return jax.shard_map(body, mesh=mesh, in_specs=in_specs, out_specs=out_specs, check_vma=False)

time: 1490 us -> 240 us (0.16)
  waiting for transfers between devices: 969 us -> 0 us
  matrix products: 241 us -> 0 us
  Pallas kernels: 0 us -> 223 us
  local copies, waits for them, and re-layouts: 139 us -> 12.7 us
  other arithmetic: 66 us -> 2.58 us
  blocking collectives: 40.6 us -> 0 us
  between operations: 16.4 us -> 1.36 us
    reduce_scatter x5 -> x0, waiting for transfers between devices: 413 us -> none  [the longest x1 95.5 us: shards(): lax.psum_scatter(grad_w_down, ('ctx', 'wsh'), scatter_dimension=0, tiled=...]
    unnamed x21 -> x0, waiting for transfers between devices: 405 us -> none
    dot_general x133 -> x0, matrix products: 241 us -> none  [the longest x55 135 us: dot_last(): lax.dot_general(left, right, (((1,), (1,)), ((), ())), preferred_element_...]
    pallas_call x0 -> x1, Pallas kernels: none -> 223 us  [layer_call(): pl.pallas_call(body, out_shape=[jax.ShapeDtypeStruct(shape, WIDE) for sha...]
    all_gather x2 -> x0, waiting for transfers between devices: 121 us -> none  [the longest x1 87.8 us: shards(): keyval_all = lax.all_gather(keyval_own, 'ctx', axis=1, tiled=True)]
    unnamed x99 -> x30, local copies, waits for them, and re-layouts: 58.2 us -> 9.09 us
    unnamed x1 -> x0, blocking collectives: 40.6 us -> none
    squeeze x33 -> x0, local copies, waits for them, and re-layouts: 34.7 us -> none  [the longest x16 19.1 us: shards(): self_out, self_lse = lax.map(self_forward, (query_heads, keyval_all))]
  transfers between devices with their start and end apart: 15 -> 0, of which waited for: 14 -> 0; matrix products, arithmetic and copies ran while one was open for 15% -> 0% of each run, Pallas kernels for 0% -> 0%
where the time goes in v1:
time: 240 us
  Pallas kernels  223 us (93%)
  local copies, waits for them, and re-layouts  12.7 us (5%)
  other arithmetic  2.58 us (1%)
    pallas_call x1, Pallas kernels, layer_call(): pl.pallas_call(body, out_shape=[jax.ShapeDtypeStruct(shape, WIDE) for sha...  223 us
    unnamed x30, local copies, waits for them, and re-layouts  9.09 us

profile of v1, /device:TPU:0, one launch (start us, length us, event | category | flops | bytes accessed | tf_op | source)
XLA Modules:
  0.0 240.0 jit_solution(10499751469618431397)
XLA Ops:
  0.6 1.3 select_reduce_fusion.args_0_
  1.9 0.7 compare_bitcast_fusion
  2.6 0.1 copy.30
  3.4 0.6 or_select_fusion.args_2_
  4.0 223.4 %layer.1 = (f32[384,512]{1,0:T(8,128)}, f32[384,512]{1,0:T(8,128)}, f32[128,512]{1,0:T(8,128)}, f32[32,1536]{1,0:T(8,128)}, f32[32,512]{1,0:T(8,128)}, /*index=5...) custom-call(s32[24]{0:T(128)} %select_reduce_fusion.args_0_, ...), custom_call_target="tpu_custom_call" | custom-call | tf_op jit(solution)/shard_map/layer/pallas_call | solution.py:944
  227.4 0.0 copy-start
  227.4 0.0 copy-start.3
  227.4 0.0 copy-start.4
  227.4 0.9 slice.11
  228.3 0.0 copy-start.8
  228.3 0.7 constant_dynamic-slice_fusion.1
  229.0 0.7 slice.10
  229.7 0.6 constant_dynamic-slice_fusion
  230.3 0.7 slice_bitcast_fusion
  231.1 0.6 dynamic_slice.9
  231.6 0.0 copy-start.7
  231.7 0.0 copy-start.5
  231.7 0.0 copy-start.6
  231.7 0.0 copy-start.2
  231.7 2.1 copy.43
  233.8 0.0 copy-done
  233.8 0.0 copy-start.1
  233.8 0.9 copy.44
  234.7 0.0 copy-done.3
  234.7 0.7 copy.45
  235.4 0.0 copy-done.4
  235.4 0.7 copy.46
  236.1 0.0 copy-done.8
  236.1 0.6 copy.47
  236.7 0.0 copy-done.7
  236.7 0.6 copy.48
  237.3 0.0 copy-done.5
  237.3 0.7 copy.49
  238.0 0.0 copy-done.6
  238.0 0.6 copy.50
  238.6 0.0 copy-done.2
  238.6 0.7 copy.51
  239.3 0.0 copy-done.1
  239.3 0.7 copy.52
  (2 shorter events, 0.0 us)
Async XLA Ops:
  227.4 6.4 %copy-start = (f32[384,512]{1,0:T(8,128)S(1)}, f32[384,512]{1,0:T(8,128)}, u32[]{:S(2)}) copy-start(f32[384,512]{1,0:T(8,128)} %get-tuple-element.25) | copy-start | bytes 2359300
  227.4 7.3 %copy-start.3 = (f32[128,512]{1,0:T(8,128)S(1)}, f32[128,512]{1,0:T(8,128)}, u32[]{:S(2)}) copy-start(f32[128,512]{1,0:T(8,128)} %get-tuple-element.26) | copy-start | bytes 786436
  227.4 8.0 %copy-start.4 = (f32[32,1536]{1,0:T(8,128)S(1)}, f32[32,1536]{1,0:T(8,128)}, u32[]{:S(2)}) copy-start(f32[32,1536]{1,0:T(8,128)} %get-tuple-element.51) | copy-start | bytes 589828
  228.3 7.8 %copy-start.8 = (f32[32,512]{1,0:T(8,128)S(1)}, f32[32,512]{1,0:T(8,128)}, u32[]{:S(2)}) copy-start(f32[32,512]{1,0:T(8,128)} %get-tuple-element.52) | copy-start | bytes 196612
  231.6 5.0 %copy-start.7 = (f32[32,512]{1,0:T(8,128)S(1)}, f32[32,512]{1,0:T(8,128)}, u32[]{:S(2)}) copy-start(f32[32,512]{1,0:T(8,128)} %get-tuple-element.53) | copy-start | bytes 196612
  231.7 5.7 %copy-start.5 = (f32[32,1024]{1,0:T(8,128)S(1)}, f32[32,1024]{1,0:T(8,128)}, u32[]{:S(2)}) copy-start(f32[32,1024]{1,0:T(8,128)} %get-tuple-element.54) | copy-start | bytes 393220
  231.7 6.3 %copy-start.6 = (f32[32,512]{1,0:T(8,128)S(1)}, f32[32,512]{1,0:T(8,128)}, u32[]{:S(2)}) copy-start(f32[32,512]{1,0:T(8,128)} %get-tuple-element.55) | copy-start | bytes 196612
  231.7 7.0 %copy-start.2 = (f32[32,2048]{1,0:T(8,128)S(1)}, f32[32,2048]{1,0:T(8,128)}, u32[]{:S(2)}) copy-start(f32[32,2048]{1,0:T(8,128)} %get-tuple-element.56) | copy-start | bytes 786436
  233.8 5.5 %copy-start.1 = (f32[128,512]{1,0:T(8,128)S(1)}, f32[128,512]{1,0:T(8,128)}, u32[]{:S(2)}) copy-start(f32[128,512]{1,0:T(8,128)} %get-tuple-element.57) | copy-start | bytes 786436

commit v2 on v1

--- a/solution.py
+++ b/solution.py
@@ -1,3 +1,5 @@
+import functools
+
 import jax
 import jax.numpy as jnp
 from jax import lax
@@ -24,9 +26,9 @@
 HALF = 16
 ROWS = 4
 PIECES = dict(
-    up0=1024, up1=1024, down0=1024, down1=1024, cross=1024, out=512, ckv=1024, qkv0=768, qkv1=768
+    up0=1024, up1=1024, down0=1024, down1=1024, cross=1024, out=512, ckv=1024, wq=512, wk=512, wv=512
 )
-TURNS = dict(up0=0, up1=1, down0=0, down1=1, cross=0, out=1, ckv=1, qkv0=0, qkv1=1)
+TURNS = dict(up0=0, up1=0, down0=0, down1=1, cross=0, out=1, ckv=1, wq=2, wk=2, wv=2)
 FEW_ROWS = 24
 
 
@@ -74,7 +76,7 @@
     return jnp.where(rows <= cols, scores, NEG_FILL)
 
 
-def hide_prompt(scores, lim_ref, tile, chunk, prompt_blocks):
+def hide_prompt(scores, offset_ref, open_ref, tile, chunk, prompt_blocks):
     span = TILE // BLK
     rows = lax.broadcasted_iota(jnp.int32, (BLK, BLK), 0)
     columns = []
@@ -82,7 +84,9 @@
         pieces = []
         for k_sub in range(span):
             key_block = chunk * span + k_sub
-            limit = lim_ref[tile * span + q_sub - prompt_blocks, key_block] - key_block * BLK
+            opened = open_ref[tile * span + q_sub - prompt_blocks, key_block]
+            opened = jnp.where(key_block == 0, 1, opened)
+            limit = jnp.where(opened > 0, offset_ref[0], 0) - key_block * BLK
             part = scores[k_sub * BLK : (k_sub + 1) * BLK, q_sub * BLK : (q_sub + 1) * BLK]
             pieces.append(jnp.where(rows < limit, part, NEG_FILL))
         columns.append(jnp.concatenate(pieces, axis=0))
@@ -128,6 +132,7 @@
         self.core_peer = (1 - self.grp, ctx, self.wsh)
         self.wsh_peer = (self.grp, ctx, 1 - self.wsh)
         self.col_peer = self.at_row_col(self.row, 1 - self.col)
+        self.cross_peer = (self.grp, self.row * 2 + 1 - self.col, 1 - self.wsh)
         self.rows_by_step = [lax.rem(self.row + step, ROWS) for step in range(ROWS)]
         self.row_peers = [self.at_row_col(row, self.col) for row in self.rows_by_step]
         near = self.row + 1 - 2 * lax.rem(self.row, 2)
@@ -143,52 +148,33 @@
 
     def greet(self):
         barrier = pltpu.get_barrier_semaphore()
-        targets = [self.core_peer, self.wsh_peer] + self.ctx_peers[1:]
+        targets = [self.core_peer, self.wsh_peer, self.cross_peer] + self.ctx_peers[1:]
         for target in targets:
             pl.semaphore_signal(barrier, inc=1, device_id=target, device_id_type=MESH_ID)
-        pl.semaphore_wait(barrier, len(targets))
+        return len(targets)
 
 
 class Exchange:
-    def __init__(self, spot, source, target, sems):
-        self.spot, self.source, self.target, self.sems = spot, source, target, sems
-        self.copies = []
-
-    def start(self):
+    def __init__(self, spot, source, target, sems, cuts):
+        self.spot, self.source, self.target, self.sems, self.cuts = spot, source, target, sems, cuts
+        self.copies = [[] for _ in cuts]
+
+    def start(self, part=0):
         spot, own_blocks = self.spot, self.source.shape[1]
-        here = pl.ds(spot.ctx * own_blocks, own_blocks)
+        first, count, rows = self.cuts[part]
+        here = (pl.ds(spot.ctx * own_blocks + first, count), rows)
+        there = (pl.ds(first, count), rows)
         for step in range(1, HEADS):
             copy = remote(
-                self.source.at[spot.ctx_by_step[step]], self.target.at[here],
-                self.sems.at[0, step], self.sems.at[1, step], spot.ctx_peers[step],
+                self.source.at[(spot.ctx_by_step[step],) + there], self.target.at[here],
+                self.sems.at[0, step, part], self.sems.at[1, step, part], spot.ctx_peers[step],
             )
             copy.start()
-            self.copies.append(copy)
-        self.target[here] = self.source[spot.ctx]
-
-    def wait(self):
-        for copy in self.copies:
-            copy.wait()
-
-
-class Spread:
-    def __init__(self, spot, source, target, sems):
-        self.spot, self.source, self.target, self.sems = spot, source, target, sems
-        self.copies = []
-
-    def start(self):
-        spot = self.spot
-        for step in range(1, HEADS):
-            copy = remote(
-                self.source, self.target.at[spot.ctx],
-                self.sems.at[0, step], self.sems.at[1, step], spot.ctx_peers[step],
-            )
-            copy.start()
-            self.copies.append(copy)
-        self.target[pl.ds(spot.ctx, 1)] = self.source[...][None]
-
-    def wait(self):
-        for copy in self.copies:
+            self.copies[part].append(copy)
+        self.target[here] = self.source[(spot.ctx,) + there]
+
+    def wait(self, part=0):
+        for copy in self.copies[part]:
             copy.wait()
 
 
@@ -211,6 +197,18 @@
             copy.wait()
         self.copies = []
 
+    def send_rows(self):
+        spot = self.spot
+        for step in range(1, ROWS):
+            self.copy(
+                2 + step, self.turn_land.at[spot.rows_by_step[step]],
+                self.row_land.at[step - 1], spot.row_peers[step],
+            )
+
+    def steps(self, stage):
+        while self.stage < stage:
+            self.step()
+
     def step(self):
         spot, part = self.spot, self.part
         own = spot.grp
@@ -219,12 +217,32 @@
         elif self.stage == 1:
             self.finish()
             part[own] = plus(part[own], self.core_land[...]).astype(LOW)
-            if self.turn == 0:
+            if self.turn == 2:
+                col, wsh = spot.col, spot.wsh
+                ways = [
+                    (spot.wsh_peer, col, 1 - wsh),
+                    (spot.col_peer, 1 - col, wsh),
+                    (spot.cross_peer, 1 - col, 1 - wsh),
+                ]
+                for way, (target, to_col, to_wsh) in enumerate(ways):
+                    self.copy(
+                        (1, 2, 6)[way], part.at[own, :, to_col, to_wsh], self.hop_land.at[way],
+                        target,
+                    )
+            elif self.turn == 0:
                 self.copy(1, part.at[own, :, :, 1 - spot.wsh], self.hop_land, spot.wsh_peer)
             else:
                 self.copy(1, part.at[own, :, 1 - spot.col], self.hop_land, spot.col_peer)
         elif self.stage == 2:
             self.finish()
+            if self.turn == 2:
+                total = part[own, :, spot.col, spot.wsh].astype(WIDE)
+                for way in range(3):
+                    total = total + self.hop_land[way].astype(WIDE)
+                self.turn_land[...] = total.astype(LOW)
+                self.send_rows()
+                self.stage = 4
+                return
             if self.turn == 0:
                 mine = part[own, :, :, spot.wsh]
                 away, target = 1 - spot.col, spot.col_peer
@@ -237,11 +255,7 @@
             self.finish()
             keep = spot.col if self.turn == 0 else spot.wsh
             self.turn_land[...] = plus(self.turn_sum[:, keep], self.turn_land[...]).astype(LOW)
-            for step in range(1, ROWS):
-                self.copy(
-                    2 + step, self.turn_land.at[spot.rows_by_step[step]],
-                    self.row_land.at[step - 1], spot.row_peers[step],
-                )
+            self.send_rows()
         elif self.stage == 4:
             self.finish()
             total = self.turn_land[spot.row].astype(WIDE)
@@ -255,7 +269,7 @@
                 )
                 out_ref[here] = total[:, at : at + width]
                 at += width
-                self.copy(6 + index, out_ref.at[here], out_ref.at[here], spot.core_peer)
+                self.copy(7 + index, out_ref.at[here], out_ref.at[here], spot.core_peer)
         elif self.stage == 5:
             self.finish()
         self.stage += 1
@@ -263,14 +277,15 @@
 
 def layer_kernel(
     prompt_blocks,
-    inv_ref, deal_ref, lim_ref, tokens_ref, memory_ref, cot_ref,
+    deal_ref, offset_ref, open_ref, tokens_ref, memory_ref, cot_ref,
     w_qkv_hbm, w_out_hbm, w_cq_hbm, w_ckv_hbm, w_cout_hbm, w_up_hbm, w_down_hbm,
     b_up_ref, gains_ref, biases_ref,
     output_ref, g_stream_ref, g_memory_ref, o_qkv_ref, o_out_ref, o_cq_ref, o_ckv_ref, o_cout_ref,
-    o_up_ref, o_down_ref, few_out_ref,
+    o_up_ref, o_down_ref, o_b_up_ref, o_gains_ref, o_biases_ref,
     refs,
 ):
     spot = Spot()
+    greeted = spot.greet()
     row_count, width = tokens_ref.shape
     own_blocks = row_count // BLK
     head = width // HEADS
@@ -305,8 +320,9 @@
         cross=[(o_cout_ref, 0, 0, 512), (o_cq_ref, 0, 0, 512)],
         out=[(o_out_ref, 0, 0, 512)],
         ckv=[(o_ckv_ref, 0, 0, 1024)],
-        qkv0=[(o_qkv_ref, 0, 0, 768)],
-        qkv1=[(o_qkv_ref, 0, 768, 768)],
+        wq=[(o_qkv_ref, 0, 0, 512)],
+        wk=[(o_qkv_ref, 0, 512, 512)],
+        wv=[(o_qkv_ref, 0, 1024, 512)],
     )
     piece = Bag(
         {
@@ -338,6 +354,10 @@
     loads.w_qkv.wait()
     zeros_row = jnp.zeros((1, width), WIDE)
     projected_bias = jnp.concatenate([bias(0), zeros_row, bias(1)], axis=1)
+    to_heads_copy = Exchange(
+        spot, send_ref, refs.head_land, refs.to_heads_sem,
+        [(block, 1, slice(0, 3 * head)) for block in range(own_blocks)],
+    )
     for block in range(own_blocks):
         rows = slice(block * BLK, (block + 1) * BLK)
         projected = (nn(tokens_ref[rows, :], refs.w_qkv[...]) + projected_bias).astype(LOW)
@@ -347,12 +367,27 @@
             for kind in range(3):
                 at = kind * width + h * head
                 send_ref[h, block, kind * head : (kind + 1) * head, :] = turned[at : at + head]
-    spot.greet()
-    to_heads_copy = Exchange(spot, send_ref, refs.head_land, refs.to_heads_sem)
-    to_heads_copy.start()
-    to_heads_copy.wait()
-    spread = Spread(spot, memory_ref, refs.memory_all, refs.spread_sem)
-    spread.start()
+        if block == 0:
+            pl.semaphore_wait(pltpu.get_barrier_semaphore(), greeted)
+        to_heads_copy.start(block)
+    inv_ref = refs.inverse
+    for pos in range(blocks):
+        row = jnp.int32(0)
+        for other in range(1, blocks):
+            row = jnp.where(deal_ref[other] == pos, other, row)
+        inv_ref[pos] = row
+    for block in range(own_blocks):
+        to_heads_copy.wait(block)
+    all_ref = refs.memory_all
+    spread = []
+    for step in range(1, ROWS):
+        copy = remote(
+            memory_ref, all_ref.at[spot.col, spot.row],
+            refs.spread_sem.at[0, step], refs.spread_sem.at[1, step], spot.row_peers[step],
+        )
+        copy.start()
+        spread.append(copy)
+    all_ref[spot.col, spot.row] = memory_ref[...]
 
     q_ref, kv_ref = refs.q, refs.kv
     no_head = jnp.zeros((head, BLK), LOW)
@@ -365,7 +400,6 @@
         qt_ref[:, at] = block[:head]
         kt_ref[:, at] = block[head : 2 * head]
         vt_ref[:, at] = block[2 * head :]
-        q_ref[at, :] = swap(jnp.concatenate([block[:head], no_head], axis=0))
         kv_ref[at, :] = swap(block[head:])
 
     def tile_spans(tile, chunk_step, state):
@@ -376,7 +410,7 @@
             0,
             first,
             lambda c, s: chunk_step(
-                c, s, lambda x, cc: hide_prompt(x, lim_ref, tile, cc, prompt_blocks)
+                c, s, lambda x, cc: hide_prompt(x, offset_ref, open_ref, tile, cc, prompt_blocks)
             ),
             state,
         )
@@ -385,45 +419,53 @@
         here = pl.ds(pl.multiple_of(tile * TILE, TILE), TILE)
         queries = jnp.concatenate([qt_ref[:, here], no_tile], axis=0)
 
-        def chunk_step(chunk, state, hide):
-            top, total, mixed = state
+        def top_step(chunk, top, hide):
             there = pl.ds(pl.multiple_of(chunk * TILE, TILE), TILE)
             scores = hide(nn(kv_ref[there, :], queries), chunk)
-            new_top = jnp.maximum(top, jnp.max(scores, axis=0, keepdims=True))
-            weights = jnp.exp(scores - new_top)
-            fade = jnp.exp(top - new_top)
-            total = total * fade + jnp.sum(weights, axis=0, keepdims=True)
-            mixed = mixed * fade + nn(vt_ref[:, there], weights.astype(LOW))
-            return new_top, total, mixed
-
-        top, total, mixed = tile_spans(
-            tile,
-            chunk_step,
-            (
-                jnp.full((1, TILE), NEG_FILL, WIDE),
-                jnp.zeros((1, TILE), WIDE),
-                jnp.zeros((head, TILE), WIDE),
-            ),
+            return jnp.maximum(top, jnp.max(scores.reshape(TILE // 8, 8, TILE), axis=0))
+
+        top = tile_spans(tile, top_step, jnp.full((8, TILE), NEG_FILL, WIDE))
+        top = jnp.max(top, axis=0, keepdims=True)
+
+        def chunk_step(chunk, state, hide):
+            total, mixed = state
+            there = pl.ds(pl.multiple_of(chunk * TILE, TILE), TILE)
+            weights = jnp.exp(hide(nn(kv_ref[there, :], queries), chunk) - top)
+            total = total + jnp.sum(weights.reshape(TILE // 8, 8, TILE), axis=0)
+            return total, mixed + nn(vt_ref[:, there], weights.astype(LOW))
+
+        total, mixed = tile_spans(
+            tile, chunk_step, (jnp.zeros((8, TILE), WIDE), jnp.zeros((head, TILE), WIDE))
         )
+        total = jnp.sum(total, axis=0, keepdims=True)
         exact = mixed / total
         for sub in range(TILE // BLK):
             exact_ref[tile * (TILE // BLK) + sub] = exact[:, sub * BLK : (sub + 1) * BLK]
         lse_ref[:, here] = top + jnp.log(total)
         return carry
 
-    lax.fori_loop(0, tiles, forward_tile, 0)
+    lax.fori_loop(0, tiles - 2, forward_tile, 0)
+    for copy in spread:
+        copy.wait()
+    spread_side = remote(
+        all_ref.at[spot.col], all_ref.at[spot.col],
+        refs.spread_sem.at[0, 0], refs.spread_sem.at[1, 0], spot.col_peer,
+    )
+    spread_side.start()
+    lax.fori_loop(tiles - 2, tiles, forward_tile, 0)
     mixed_ref = refs.mixed_send
     for row in range(blocks):
         mixed_ref[row // own_blocks, row % own_blocks] = exact_ref[deal_ref[row]].astype(LOW)
-    from_heads_copy = Exchange(spot, mixed_ref, refs.mixed_land, refs.from_heads_sem)
+    all_blocks = [(0, own_blocks, slice(0, head))]
+    from_heads_copy = Exchange(spot, mixed_ref, refs.mixed_land, refs.from_heads_sem, all_blocks)
     from_heads_copy.start()
 
     ck_ref, cv_ref, ckt_ref, cvt_ref = refs.ck, refs.cv, refs.ckt, refs.cvt
     loads.w_ckv.wait()
-    spread.wait()
+    spread_side.wait()
     for part in range(HEADS):
         rows = slice(part * mem_rows, (part + 1) * mem_rows)
-        both = nn(refs.memory_all[part], refs.w_ckv[...])
+        both = nn(all_ref[part % 2, part // 2], refs.w_ckv[...])
         keys = both[:, :width].astype(LOW)
         values = (both[:, width:] + bias(5)).astype(LOW)
         ck_ref[rows, :] = keys
@@ -464,7 +506,6 @@
     lax.fori_loop(0, own_blocks, first_norm, 0)
 
     pair_width = 2 * head
-    scores_ref, weights_ref = refs.scores, refs.weights
     cross_exact_ref, cross_lse_ref = refs.cross_exact, refs.cross_lse
     steps = mem_total // STEP
 
@@ -484,24 +525,27 @@
 
             def first_pass(step, top):
                 scores = nn(ck_ref[step_at(step), lanes], queries)
-                scores_ref[step_at(step), :] = scores
-                return jnp.maximum(top, jnp.max(scores, axis=0, keepdims=True))
+                return jnp.maximum(top, jnp.max(scores.reshape(STEP // 8, 8, row_count), axis=0))
 
             top = lax.fori_loop(
-                0, steps, first_pass, jnp.full((1, row_count), NEG_FILL, WIDE), unroll=True
+                0, steps, first_pass, jnp.full((8, row_count), NEG_FILL, WIDE), unroll=True
             )
-
-            def second_pass(step, total):
-                weights = jnp.exp(scores_ref[step_at(step), :] - top)
-                weights_ref[step_at(step), :] = weights.astype(LOW)
-                return total + jnp.sum(weights, axis=0, keepdims=True)
-
-            total = lax.fori_loop(
-                0, steps, second_pass, jnp.zeros((1, row_count), WIDE), unroll=True
+            top = jnp.max(top, axis=0, keepdims=True)
+
+            def second_pass(step, state):
+                total, mixed = state
+                weights = jnp.exp(nn(ck_ref[step_at(step), lanes], queries) - top)
+                total = total + jnp.sum(weights.reshape(STEP // 8, 8, row_count), axis=0)
+                return total, mixed + nn(cvt_ref[at, step_at(step)], weights.astype(LOW))
+
+            total, mixed = lax.fori_loop(
+                0, steps, second_pass,
+                (jnp.zeros((8, row_count), WIDE), jnp.zeros((head, row_count), WIDE)), unroll=True,
             )
+            total = jnp.sum(total, axis=0, keepdims=True)
             across = slice(side * row_count, (side + 1) * row_count)
             cross_lse_ref[pl.ds(pair, 1), across] = top + jnp.log(total)
-            cross_exact_ref[at, :] = nn(cvt_ref[at, :], weights_ref[...]) / total
+            cross_exact_ref[at, :] = mixed / total
         return carry
 
     lax.fori_loop(0, pairs, cross_forward, 0)
@@ -578,6 +622,8 @@
         put_rows(ups[chunk // 2], grad_up, (chunk % 2) * width)
         if chunk % 2 == 1:
             ups[chunk // 2].step()
+        if chunk == 2:
+            piece.up0.step()
         grad_down = nn(swap(hidden_ref[chunk]), low_third_ref[...])
         split = grad_down.astype(LOW).reshape(2, 2, 4, 2, HALF, width)
         for part in range(4):
@@ -611,12 +657,11 @@
     few(14, sums[1])
     few(13, sums[2])
     put_rows(piece.cross, nn(swap(cross_low_ref[...]), low_third_ref[...]), 0)
-    piece.up0.step()
     piece.up1.step()
-
-    dcqt_ref, dsend_ref, dland_ref = refs.dcqt, w_up_ref, refs.dkv_land
-    side_width = ROWS * 2 * pair_width
-    dkv_copies = []
+    piece.down0.step()
+    piece.down1.step()
+
+    dcqt_ref = refs.dcqt
     for pair in range(pairs):
         lanes = slice(pair * pair_width, (pair + 1) * pair_width)
         low_half = slice(pair * pair_width, pair * pair_width + head)
@@ -637,32 +682,13 @@
             weights = jnp.exp(nn(ck_ref[there, lanes], queries_t) - lse)
             grad_weights = nn(cv_ref[there, lanes], upstream_t)
             grad_scores = (weights * (grad_weights - delta)).astype(LOW)
-            grad_keys = nn(grad_scores, queries).astype(LOW)
-            grad_values = nn(weights.astype(LOW), upstream).astype(LOW)
-            for sub in range(STEP // mem_rows):
-                rows = slice(sub * mem_rows, (sub + 1) * mem_rows)
-                at = sub * side_width + step * 2 * pair_width
-                at = pl.ds(pl.multiple_of(at, pair_width), 2 * pair_width)
-                dsend_ref[pair * mem_rows : (pair + 1) * mem_rows, at] = jnp.concatenate(
-                    [grad_keys[rows], grad_values[rows]], axis=1
-                )
+            ck_ref[there, lanes] = nn(grad_scores, queries).astype(LOW)
+            cv_ref[there, lanes] = nn(weights.astype(LOW), upstream).astype(LOW)
             dcqt_ref[low_half, :] += nn(ckt_ref[low_half, there], grad_scores[:, :row_count])
             dcqt_ref[high_half, :] += nn(ckt_ref[high_half, there], grad_scores[:, row_count:])
             return carry
 
         lax.fori_loop(0, steps, backward_step, 0)
-        copy = remote(
-            dsend_ref.at[
-                pl.ds(pair * mem_rows, mem_rows),
-                pl.ds(pl.multiple_of((1 - spot.col) * side_width, side_width), side_width),
-            ],
-            dland_ref.at[pair],
-            refs.dkv_sem.at[0, pair], refs.dkv_sem.at[1, pair], spot.col_peer,
-        )
-        copy.start()
-        dkv_copies.append(copy)
-        (downs if pair < 2 else ups)[pair % 2].step()
-
     upstream_send = refs.mixed_send
 
     def first_back(block, sums):
@@ -690,19 +716,44 @@
     few(10, sums[1])
     few(9, sums[2])
     few(11, sums[3])
-    up_heads_copy = Exchange(spot, upstream_send, refs.up_land, refs.up_heads_sem)
+    up_heads_copy = Exchange(spot, upstream_send, refs.up_land, refs.up_heads_sem, all_blocks)
     up_heads_copy.start()
     turned_ref[...] = swap(low_one_ref[...])
     put_rows(piece.cross, nn(turned_ref[...], dco_ref[...]), width)
-    piece.cross.step()
+    piece.cross.steps(1)
     put_rows(piece.out, nn(attended_t_ref[...], low_third_ref[...]), 0)
-    piece.out.step()
-    piece.down0.step()
-    piece.down1.step()
-    piece.cross.step()
+    piece.out.steps(1)
+    piece.up0.steps(3)
+    for part in range(HEADS):
+        rows = slice(part * mem_rows, (part + 1) * mem_rows)
+        ckt_ref[:, rows] = swap(all_ref[part % 2, part // 2])
+        grad = nt(ck_ref[rows, :], refs.w_ckv[:, :width]) + nt(cv_ref[rows, :], refs.w_ckv[:, width:])
+        w_up_ref[
+            (part // 2) * mem_rows : (part // 2 + 1) * mem_rows,
+            (part % 2) * width : (part % 2 + 1) * width,
+        ] = grad.astype(LOW)
+    g_land = refs.memory_land
+    other_side = pl.ds(pl.multiple_of((1 - spot.col) * width, width), width)
+    own_side = pl.ds(pl.multiple_of(spot.col * width, width), width)
+    memory_copy = remote(
+        w_up_ref.at[:, other_side], g_land, refs.memory_sem.at[0, 0], refs.memory_sem.at[1, 0],
+        spot.col_peer,
+    )
+    memory_copy.start()
+    piece.cross.steps(2)
+    piece.out.steps(2)
+    put_rows(piece.ckv, nn(ckt_ref[...], ck_ref[...]), 0)
+    put_rows(piece.ckv, nn(ckt_ref[...], cv_ref[...]), width)
+    few(12, column_sums(cv_ref[...]))
+    piece.ckv.steps(1)
+    for pos in range(blocks):
+        at = slice(pos * BLK, (pos + 1) * BLK)
+        q_ref[at, :] = swap(jnp.concatenate([qt_ref[:, at], no_head], axis=0))
+    piece.up1.steps(3)
+    piece.down1.steps(3)
     up_heads_copy.wait()
-    piece.up0.step()
-    piece.up1.step()
+    piece.ckv.steps(2)
+    piece.down0.steps(3)
 
     upq_ref, upt_ref = refs.up, refs.upt
     dkv_ref, dqt_ref = refs.dkv, refs.dqt
@@ -742,65 +793,102 @@
         return carry
 
     lax.fori_loop(0, tiles // 2, backward_tile, 0)
-    piece.out.step()
-    piece.cross.step()
-    piece.down0.step()
-    piece.down1.step()
-    dsum_ref, drow_ref = refs.dkv_sum, refs.dkv_row
-    for copy in dkv_copies:
-        copy.wait()
-    own_side = pl.ds(pl.multiple_of(spot.col * side_width, side_width), side_width)
-    for pair in range(pairs):
-        own_rows = slice(pair * mem_rows, (pair + 1) * mem_rows)
-        both = plus(dsend_ref[own_rows, own_side], dland_ref[pair]).astype(LOW)
-        for row in range(ROWS):
-            dsum_ref[row, pair] = both[:, row * 2 * pair_width : (row + 1) * 2 * pair_width]
-    dkv_copies = []
+    memory_copy.wait()
+    g_land[...] = plus(w_up_ref[:, own_side], g_land[...]).astype(LOW)
+    memory_copies = []
     for step in range(1, ROWS):
         copy = remote(
-            dsum_ref.at[spot.rows_by_step[step]], drow_ref.at[step - 1],
-            refs.dkv_sem.at[0, 3 + step], refs.dkv_sem.at[1, 3 + step], spot.row_peers[step],
+            g_land.at[pl.ds(spot.rows_by_step[step] * mem_rows, mem_rows)], refs.memory_row.at[step - 1],
+            refs.memory_sem.at[0, step], refs.memory_sem.at[1, step], spot.row_peers[step],
         )
         copy.start()
-        dkv_copies.append(copy)
-    lax.fori_loop(tiles // 2, tiles - 1, backward_tile, 0)
-    piece.out.step()
-    piece.cross.step()
+        memory_copies.append(copy)
+    piece.up0.steps(4)
+    piece.up1.steps(4)
+    piece.down1.steps(4)
+    piece.cross.steps(3)
+    lax.fori_loop(tiles // 2, tiles - 2, backward_tile, 0)
+    piece.down0.steps(4)
+    piece.out.steps(3)
+    piece.cross.steps(4)
+    lax.fori_loop(tiles - 2, tiles - 1, backward_tile, 0)
+    piece.out.steps(4)
+    piece.ckv.steps(3)
+    piece.up0.steps(5)
+    piece.up1.steps(5)
     lax.fori_loop(tiles - 1, tiles, backward_tile, 0)
 
+    piece.ckv.steps(4)
     back_send = refs.head_send
+    back_copy = Exchange(
+        spot, back_send, refs.head_land, refs.back_sem,
+        [(0, own_blocks, slice(kind * head, (kind + 1) * head)) for kind in range(3)],
+    )
     for row in range(blocks):
-        pos = deal_ref[row]
-        to = (row // own_blocks, row % own_blocks)
-        back_send[to[0], to[1], :head] = dqt_ref[pos]
-        back_send[to[0], to[1], head:] = dkv_ref[pos].T.astype(LOW)
-    back_copy = Exchange(spot, back_send, refs.head_land, refs.back_sem)
-    back_copy.start()
-
-    for copy in dkv_copies:
+        back_send[row // own_blocks, row % own_blocks, :head] = dqt_ref[deal_ref[row]]
+    back_copy.start(0)
+    for row in range(blocks):
+        back_send[row // own_blocks, row % own_blocks, head:] = dkv_ref[deal_ref[row]].T.astype(LOW)
+    back_copy.start(1)
+    back_copy.start(2)
+
+    ones = jnp.ones((8, BLK), LOW)
+    query_sums = jnp.zeros((8, head), WIDE)
+    both_sums = jnp.zeros((1, 2 * head), WIDE)
+    for pos in range(blocks):
+        query_sums = query_sums + nt(ones, dqt_ref[pos])
+        both_sums = both_sums + column_sums(dkv_ref[pos])
+    own_lanes = lax.broadcasted_iota(jnp.int32, (1, width), 1) // head == spot.ctx
+    few(7, jnp.where(own_lanes, jnp.concatenate([query_sums[:1]] * HEADS, axis=1), 0.0))
+    few(8, jnp.where(own_lanes, jnp.concatenate([both_sums[:, head:]] * HEADS, axis=1), 0.0))
+
+    def few_copy(step):
+        return remote(
+            few_ref.at[step], refs.few_land.at[step],
+            refs.few_sem.at[0, step], refs.few_sem.at[1, step], spot.few_peers[step],
+        )
+
+    few_copy(0).start()
+    finishing = [
+        (piece.down1, piece.down0), (piece.cross, piece.out), (piece.ckv,), (), (),
+    ]
+    for step in range(5):
+        for item in finishing[step]:
+            item.steps(5)
+        few_copy(step).wait()
+        total = few_ref[step] + refs.few_land[step]
+        if step < 4:
+            few_ref[step + 1] = total
+            few_copy(step + 1).start()
+        else:
+            refs.few_total[...] = total
+    own_shard = spot.ctx * 2 + spot.wsh
+    total = refs.few_total[...]
+    part, long_part = width // SHARDS, hidden_width // SHARDS
+    picked, long_picked = total[:, :part], total[:1, :long_part]
+    for shard in range(1, SHARDS):
+        picked = jnp.where(own_shard == shard, total[:, shard * part : (shard + 1) * part], picked)
+        row, at = divmod(shard * long_part, width)
+        long_picked = jnp.where(
+            own_shard == shard, total[row : row + 1, at : at + long_part], long_picked
+        )
+    o_b_up_ref[...] = long_picked
+    o_gains_ref[...] = picked[4:7]
+    o_biases_ref[...] = picked[7:17]
+    for copy in memory_copies:
         copy.wait()
-    for pair in range(pairs):
-        total = dsum_ref[spot.row, pair].astype(WIDE)
-        for step in range(ROWS - 1):
-            total = total + drow_ref[step, pair].astype(WIDE)
-        refs.dckv[:, pair * pair_width : (pair + 1) * pair_width] = total[:, :pair_width].astype(LOW)
-        at = width + pair * pair_width
-        refs.dckv[:, at : at + pair_width] = total[:, pair_width:].astype(LOW)
-    dckv = refs.dckv[...]
-    put_rows(piece.ckv, nn(swap(memory_ref[...]), dckv), 0)
-    piece.ckv.step()
-    few(12, column_sums(dckv[:, width:]))
-    g_memory_ref[...] = nt(dckv, refs.w_ckv[...])
-    piece.out.step()
-    piece.cross.step()
-    for item in ups + downs:
-        item.step()
-    piece.ckv.step()
-
-    back_copy.wait()
-    for block in range(own_blocks):
-        rows = slice(block * BLK, (block + 1) * BLK)
-        for kind in range(3):
+    total = g_land[pl.ds(spot.row * mem_rows, mem_rows), :].astype(WIDE)
+    for step in range(ROWS - 1):
+        total = total + refs.memory_row[step].astype(WIDE)
+    g_memory_ref[...] = total
+    for item in ups + downs + (piece.cross, piece.out, piece.ckv):
+        item.steps(6)
+
+    turned_ref[...] = swap(tokens_ref[...])
+    kinds = (piece.wq, piece.wk, piece.wv)
+    for kind in range(3):
+        back_copy.wait(kind)
+        for block in range(own_blocks):
             turned = jnp.concatenate(
                 [
                     refs.head_land[h * own_blocks + block, kind * head : (kind + 1) * head, :]
@@ -808,49 +896,21 @@
                 ],
                 axis=0,
             )
-            hidden_ref[kind, rows, :] = swap(turned)
-    turned_ref[...] = swap(tokens_ref[...])
-    put_rows(piece.qkv0, nn(turned_ref[...], hidden_ref[0]), 0)
-    grad_keys = nn(turned_ref[...], hidden_ref[1])
-    put_rows(piece.qkv0, grad_keys[:, : width // 2], width)
-    piece.qkv0.step()
-    put_rows(piece.qkv1, grad_keys[:, width // 2 :], 0)
-    put_rows(piece.qkv1, nn(turned_ref[...], hidden_ref[2]), width // 2)
-    piece.qkv1.step()
-    few(7, column_sums(hidden_ref[0]))
-    few(8, column_sums(hidden_ref[2]))
-
-    def few_copy(step):
-        return remote(
-            few_ref.at[step], refs.few_land.at[step],
-            refs.few_sem.at[0, step], refs.few_sem.at[1, step], spot.few_peers[step],
-        )
-
-    few_copy(0).start()
-    piece.ckv.step()
+            hidden_ref[kind, block * BLK : (block + 1) * BLK, :] = swap(turned)
+        put_rows(kinds[kind], nn(turned_ref[...], hidden_ref[kind]), 0)
+        kinds[kind].steps(1)
+        if kind > 0:
+            kinds[kind - 1].steps(2)
     grad_stream = total_ref[...]
     for kind in range(3):
+        if kind == 1:
+            kinds[2].steps(2)
         lanes = slice(kind * width, (kind + 1) * width)
         grad_stream = grad_stream + nt(hidden_ref[kind], refs.w_qkv[:, lanes])
     g_stream_ref[...] = grad_stream
-    piece.qkv0.step()
-    piece.qkv1.step()
-    for step in range(5):
-        few_copy(step).wait()
-        total = few_ref[step] + refs.few_land[step]
-        if step < 4:
-            few_ref[step + 1] = total
-            few_copy(step + 1).start()
-        else:
-            few_out_ref[...] = total
-        if step < 3:
-            piece.qkv0.step()
-            piece.qkv1.step()
-            if step < 2:
-                piece.ckv.step()
-    for name in PIECES:
-        while getattr(piece, name).stage < 6:
-            getattr(piece, name).step()
+    for stage in (3, 5, 6):
+        for item in kinds:
+            item.steps(stage)
 
 
 def layer_scratch(row_count, width, hidden_width, mem_rows):
@@ -867,7 +927,7 @@
         w_down=((hidden_width, width), LOW),
         head_send=((HEADS, own_blocks, 3 * head, BLK), LOW),
         head_land=((blocks, 3 * head, BLK), LOW),
-        memory_all=((HEADS, mem_rows, width), LOW),
+        memory_all=((2, ROWS, mem_rows, width), LOW),
         q=((tokens, 2 * head), LOW), kv=((tokens, 2 * head), LOW),
         qt=((head, tokens), LOW), kt=((head, tokens), LOW), vt=((head, tokens), LOW),
         exact=((blocks, head, BLK), WIDE), lse=((1, tokens), WIDE),
@@ -880,7 +940,6 @@
         scale_one=((row_count, 1), WIDE), scale_two=((row_count, 1), WIDE),
         low_one=((row_count, width), LOW), low_two=((row_count, width), LOW),
         cq=((row_count, width), LOW), cqt=((width, row_count), LOW),
-        scores=((mem_total, row_count), WIDE), weights=((mem_total, row_count), LOW),
         cross_exact=((width, row_count), WIDE),
         cross_lse=((HEADS // 2, 2 * row_count), WIDE),
         cross_low=((row_count, width), LOW),
@@ -890,30 +949,32 @@
         turned=((width, row_count), LOW),
         dco=((row_count, width), LOW), dcot=((width, row_count), LOW),
         dcqt=((width, row_count), WIDE),
-        dkv_land=((HEADS // 2, mem_rows, ROWS * 4 * head), LOW),
-        dkv_sum=((ROWS, HEADS // 2, mem_rows, 4 * head), LOW),
-        dkv_row=((ROWS - 1, HEADS // 2, mem_rows, 4 * head), LOW),
-        dckv=((mem_rows, 2 * width), LOW),
+        memory_land=((ROWS * mem_rows, width), LOW),
+        memory_row=((ROWS - 1, mem_rows, width), LOW),
         up_land=((blocks, head, BLK), LOW),
         up=((tokens, 2 * head), LOW), upt=((head, tokens), LOW),
         dkv=((blocks, BLK, 2 * head), WIDE), dqt=((blocks, head, BLK), LOW),
         few_sum=((5, FEW_ROWS, width), WIDE), few_land=((5, FEW_ROWS, width), WIDE),
+        few_total=((FEW_ROWS, width), WIDE),
     )
     out = {name: pltpu.VMEM(shape, kind) for name, (shape, kind) in scratch.items()}
     out.update(
-        load_sem=dma((7,)), to_heads_sem=dma((2, HEADS)), from_heads_sem=dma((2, HEADS)),
-        up_heads_sem=dma((2, HEADS)), back_sem=dma((2, HEADS)), spread_sem=dma((2, HEADS)),
-        dkv_sem=dma((2, HEADS)), few_sem=dma((2, 5)),
+        load_sem=dma((7,)), to_heads_sem=dma((2, HEADS, 3)), from_heads_sem=dma((2, HEADS, 1)),
+        up_heads_sem=dma((2, HEADS, 1)), back_sem=dma((2, HEADS, 3)), spread_sem=dma((2, ROWS)),
+        inverse=pltpu.SMEM((blocks,), jnp.int32),
+        memory_sem=dma((2, ROWS)), few_sem=dma((2, 5)),
     )
     out.update(
         pieces={
             name: dict(
                 part=pltpu.VMEM((2, ROWS, 2, 2, HALF, span), LOW),
                 core_land=pltpu.VMEM((ROWS, 2, 2, HALF, span), LOW),
-                hop_land=pltpu.VMEM((ROWS, 2, HALF, span), LOW),
+                hop_land=pltpu.VMEM(
+                    (3, ROWS, HALF, span) if TURNS[name] == 2 else (ROWS, 2, HALF, span), LOW
+                ),
                 turn_land=pltpu.VMEM((ROWS, HALF, span), LOW),
                 row_land=pltpu.VMEM((ROWS - 1, HALF, span), LOW),
-                sems=dma((2, 8)),
+                sems=dma((2, 9)),
             )
             for name, span in PIECES.items()
         }
@@ -921,7 +982,7 @@
     return out
 
 
-def layer_call(inverse, deal_ids, limits, tokens, memory, cotangent, weights, b_up, gains, biases, prompt_blocks):
+def layer_call(deal_ids, offsets, opened, tokens, memory, cotangent, weights, b_up, gains, biases, prompt_blocks):
     row_count, width = tokens.shape
     hidden_width = b_up.shape[1]
     mem_rows = memory.shape[0]
@@ -933,7 +994,8 @@
     out_shapes = [
         (row_count, width), (row_count, width), (mem_rows, width),
         (32, 3 * width), (32, width), (32, width), (32, 2 * width), (32, width),
-        (32, hidden_width), (hidden_width // SHARDS, width), (FEW_ROWS, width),
+        (32, hidden_width), (hidden_width // SHARDS, width),
+        (1, hidden_width // SHARDS), (3, width // SHARDS), (10, width // SHARDS),
     ]
 
     def body(*args):
@@ -951,35 +1013,40 @@
             collective_id=0, has_side_effects=True, vmem_limit_bytes=BIG_VMEM
         ),
         name="layer",
-    )(inverse, deal_ids, limits, tokens, memory, cotangent, *weights, b_up, gains, biases)
+    )(deal_ids, offsets, opened, tokens, memory, cotangent, *weights, b_up, gains, biases)
+
+
+def hand_out_kernel(count, *refs):
+    for index in range(count):
+        refs[count + index][...] = refs[index][...]
+
+
+def hand_out(arrays):
+    count = len(arrays)
+    vmem = pl.BlockSpec(memory_space=pltpu.VMEM)
+    return pl.pallas_call(
+        functools.partial(hand_out_kernel, count),
+        out_shape=[jax.ShapeDtypeStruct(a.shape, a.dtype) for a in arrays],
+        in_specs=[vmem] * count,
+        out_specs=[vmem] * count,
+        compiler_params=pltpu.CompilerParams(vmem_limit_bytes=BIG_VMEM),
+        name="hand_out",
+    )(*arrays)
 
 
 def layer_shards(
     stream, memory, cotangent, deal_order, offsets, context_mask,
     w_qkv, w_out, w_cq, w_ckv, w_cout, w_up, w_down, b_up, gains, biases,
 ):
-    deal_ids = deal_order[0, 0]
-    prompt_blocks = context_mask.shape[3]
-    places = jnp.arange(deal_ids.shape[0], dtype=jnp.int32)
-    inverse = jnp.sum(
-        jnp.where(deal_ids[None, :] == places[:, None], places[None, :], 0), axis=1, dtype=jnp.int32
-    )
-    blocks_open = (context_mask[0, 0] > 0) | (jnp.arange(prompt_blocks)[None, :] == 0)
-    limits = jnp.where(blocks_open, offsets[0, 0, 0], 0).astype(jnp.int32)
-    *grads, few = layer_call(
-        inverse, deal_ids, limits, stream[0, 0], memory[0, 0], cotangent[0, 0],
+    results = layer_call(
+        deal_order[0, 0], offsets[0, 0], context_mask[0, 0],
+        stream[0, 0], memory[0, 0], cotangent[0, 0],
         (w_qkv, w_out, w_cq, w_ckv, w_cout, w_up, w_down),
-        b_up[None, :], gains, biases, prompt_blocks,
-    )
-    output, grad_stream, grad_memory = grads[:3]
-    own = lax.axis_index("ctx") * 2 + lax.axis_index("wsh")
-    total_b_up = lax.dynamic_slice_in_dim(few[:4].reshape(-1), own * 128, 128)
-    total_gains = lax.dynamic_slice_in_dim(few[4:7], own * 32, 32, axis=1)
-    total_biases = lax.dynamic_slice_in_dim(few[7:17], own * 32, 32, axis=1)
-    return (
-        output[None, None], grad_stream[None, None], grad_memory[None, None],
-        *grads[3:], total_b_up, total_gains, total_biases,
-    )
+        b_up[None, :], gains, biases, context_mask.shape[3],
+    )
+    output, grad_stream, grad_memory, *grads = hand_out(results)
+    grads[7] = grads[7].reshape(-1)
+    return (output[None, None], grad_stream[None, None], grad_memory[None, None], *grads)
 
 
 def gelu_exact(values):

time: 240 us -> 206 us (0.86)
  Pallas kernels: 223 us -> 203 us
  local copies, waits for them, and re-layouts: 12.7 us -> 1.36 us
  other arithmetic: 2.58 us -> 0 us
    pallas_call x1, Pallas kernels: 223 us -> 200 us  [layer_call(): pl.pallas_call(body, out_shape=[jax.ShapeDtypeStruct(shape, WIDE) for sha...]
    unnamed x30 -> x0, local copies, waits for them, and re-layouts: 9.09 us -> none
    pallas_call x0 -> x1, Pallas kernels: none -> 3.39 us  [hand_out(): pl.pallas_call(functools.partial(hand_out_kernel, count), out_shape=[jax....]
where the time goes in v2:
time: 206 us
  Pallas kernels  203 us (99%)
    pallas_call x1, Pallas kernels, layer_call(): pl.pallas_call(body, out_shape=[jax.ShapeDtypeStruct(shape, WIDE) for sha...  200 us

profile of v2, /device:TPU:0, one launch (start us, length us, event | category | flops | bytes accessed | tf_op | source)
XLA Modules:
  0.0 206.1 jit_solution(10085977406069953522)
XLA Ops:
  1.3 1.4 copy.29.args_2_
  2.6 199.8 %layer.1 = (f32[384,512]{1,0:T(8,128)}, f32[384,512]{1,0:T(8,128)}, f32[128,512]{1,0:T(8,128)}, f32[32,1536]{1,0:T(8,128)}, f32[32,512]{1,0:T(8,128)}, /*index=5...) custom-call(s32[24]{0:T(128)} %bitcast.17, ...), custom_call_target="tpu_custom_call" | custom-call | tf_op jit(solution)/shard_map/layer/pallas_call | solution.py:1006
  202.5 3.4 %hand_out.1 = (f32[384,512]{1,0:T(8,128)}, f32[384,512]{1,0:T(8,128)}, f32[128,512]{1,0:T(8,128)}, f32[32,1536]{1,0:T(8,128)}, f32[32,512]{1,0:T(8,128)}, /*inde...) custom-call(f32[384,512]{1,0:T(8,128)} %get-tuple-element.39.refs_0_, ...), custom_call_target="tpu_custom_call" | custom-call | tf_op jit(solution)/shard_map/hand_out/pallas_call | solution.py:1027
